TPU v7x, 32 devices: a whole 2x2x4 slice. The times are simulated.
32 devices in a mesh: blk: 8 (over y, x, core), sig: 4 (over z).
Axes of the slice: x: 2, y: 2, z: 4, core: 2. Of those that a mesh axis runs over, the one named last changes fastest.
Arguments:
- coarse_fields: float32 [4096, 3, 512], P(('blk', 'sig')), may hold values from -6 to 6
- fine_fields: float32 [1024, 3, 8, 512], P(('blk', 'sig')), may hold values from -6 to 6
- owner: int32 [1024, 1], P(('blk', 'sig')), may hold values from 0 to 7, as said below
- target_tile: int32 [1024, 1], P(('blk', 'sig')), may hold values from 0 to 127, as said below
- tags: int32 [4096, 512], P(('blk', 'sig')), may hold values 0 or 1
Outputs:
- synced: float32 [4096, 3, 512], P(('blk', 'sig'))
- signature: float32 [8, 1032], P('blk')
Inputs may be any that keep to these rules, and one draw needn't show every extreme that they name: On the 32 patches of one device at most 16 name the same owner; in every sig slab some devices name one owner exactly 16 times. `target_tile`: among the patches of all devices with one sig index no owner and tile is named twice; in every sig slab one owner has all 128 of its tiles named.
All inputs are finite; a program needn't handle non-finite values. No bound on the sum of `tags` on one device may be relied on, other than what follows from the above.
Results may differ from a plain program's by a relative error of at most 0.0002.
Values sent between devices are 32-bit elements; how exact they have to be, the bound alone decides.
A program may use at most 64 MiB of HBM per device.

v0:
```python
import jax
import jax.numpy as jnp
from jax import lax
from jax.sharding import PartitionSpec as P

EDGE = 8


def indicator_of(fields):
    edge_len = fields.shape[2]
    total = jnp.zeros(fields.shape[:1] + fields.shape[2:], jnp.float32)
    for axis_number in (2, 3, 4):
        upper = lax.slice_in_dim(fields, 2, edge_len, axis=axis_number)
        lower = lax.slice_in_dim(fields, 0, edge_len - 2, axis=axis_number)
        middle = 0.5 * (upper - lower)
        widths = [(0, 0)] * 5
        widths[axis_number] = (1, 1)
        padded = jnp.pad(middle, widths)
        total = total + jnp.sum(padded * padded, axis=1)
    return total


def shards(coarse_fields, fine_fields, owner, target_tile, tags):
    patch_count = fine_fields.shape[0]
    tile_count = coarse_fields.shape[0]
    cell_count = coarse_fields.shape[2]
    edge_len = EDGE
    width = 3 * cell_count
    blocks = lax.axis_size("blk")
    slabs = lax.axis_size("sig")
    destination = owner[:, 0]
    target = target_tile[:, 0]
    child_mean = 0.125 * jnp.sum(fine_fields, axis=2)
    averaged = child_mean.reshape(patch_count, width)
    capacity = max(2, (tile_count + blocks - 1) // blocks)
    dest_match = (destination[:, None] == jnp.arange(blocks, dtype=jnp.int32)[None, :]).astype(
        jnp.int32
    )
    before = jnp.cumsum(dest_match, axis=0) - dest_match
    slot_rank = jnp.sum(before * dest_match, axis=1)
    slot_index = destination * capacity + slot_rank
    send_data = jnp.zeros((blocks * capacity, width), jnp.float32).at[slot_index].set(averaged)
    send_tiles = (
        jnp.zeros((blocks * capacity,), jnp.float32)
        .at[slot_index]
        .set((target + 1).astype(jnp.float32))
    )
    got_data, got_tiles = (
        lax.all_to_all(
            send_data.reshape(blocks, capacity, width),
            "blk",
            split_axis=0,
            concat_axis=0,
            tiled=True,
        ),
        lax.all_to_all(
            send_tiles.reshape(blocks, capacity), "blk", split_axis=0, concat_axis=0, tiled=True
        ),
    )
    tile_of_slot = got_tiles.reshape(blocks * capacity).astype(jnp.int32) - 1
    tile_of_slot = jnp.where(tile_of_slot < 0, tile_count, tile_of_slot)
    totals = (
        jnp.zeros((tile_count, width), jnp.float32)
        .at[tile_of_slot]
        .set(got_data.reshape(blocks * capacity, width), mode="drop")
    )
    covered = jnp.zeros((tile_count,), jnp.float32).at[tile_of_slot].set(1.0, mode="drop")
    flat = coarse_fields.reshape(tile_count, width)
    synced = jnp.where(covered[:, None] > 0, totals, flat)
    synced = synced.reshape(tile_count, 3, cell_count)
    indicator = indicator_of(synced.reshape(tile_count, 3, edge_len, edge_len, edge_len))
    weight = tags.reshape(tile_count, edge_len, edge_len, edge_len).astype(jnp.float32) * indicator
    part_y = jnp.sum(weight, axis=(1, 3)).reshape(tile_count * edge_len)
    part_z = jnp.sum(weight, axis=(0, 1, 2))
    sum_y, sum_z = lax.psum((part_y, part_z), "sig")
    along_y = sum_y / (edge_len * edge_len * slabs)
    along_z = sum_z / (edge_len * edge_len * tile_count * slabs)
    signature = jnp.concatenate([along_y, along_z])[None, :]
    return (synced, signature)


def solution(mesh):
    return jax.shard_map(
        shards,
        mesh=mesh,
        in_specs=(
            P(("blk", "sig"), None, None),
            P(("blk", "sig"), None, None, None),
            P(("blk", "sig"), None),
            P(("blk", "sig"), None),
            P(("blk", "sig"), None),
        ),
        out_specs=(P(("blk", "sig"), None, None), P("blk", None)),
        check_vma=False,
    )
```

profile of v0, /device:TPU:0, one launch (start us, length us, event | category | flops | bytes accessed | tf_op | source)
XLA Modules:
  0.0 48.1 jit_solution(18064527687518213806)
XLA Ops:
  0.6 0.7 %fusion.8 = s32[32,8]{1,0:T(8,128)S(1)} fusion(s32[32]{0:T(128)} %bitcast.32), kind=kLoop, calls=%fused_computation.25 | loop fusion | flops 512 | bytes 1152 | tf_op jit(solution)/shard_map/convert_element_type | solution.py:36
  1.4 0.1 reduce_window_sum.11
  1.4 0.8 %select_reduce_fusion = s32[32]{0:T(128)S(1)} fusion(s32[32,8]{1,0:T(8,128)S(1)} %reduce_window_sum.11, s32[32]{0:T(128)} %bitcast.33), kind=kLoop, calls=%fused_computation.23 | loop fusion | flops 1248 | bytes 1280 | tf_op jit(solution)/shard_map/reduce_sum | solution.py:40
  2.2 0.7 %fusion.9 = (s32[32]{0:T(128)S(1)}, f32[32]{0:T(128)S(1)}) fusion(s32[32]{0:T(128)S(1)} %select_reduce_fusion, s32[32,1]{0,1:T(1,128)} %param.7, s32[32,1]{0,1:T(1,128)} %param.8), kind=kLoop, calls=%fused_computation.32 | loop fusion | flops 224 | bytes 640 | tf_op jit(solution)/shard_map/select_n | solution.py:46
  2.9 0.7 %scatter_custom_fusion = f32[128]{0:T(128)S(1)} fusion(s32[32]{0:T(128)S(1)} %get-tuple-element.14, f32[32]{0:T(128)S(1)} %get-tuple-element.15, f32[]{:T(128)} %constant.11.clone.1), kind=kCustom, calls=%fused_computation.40 | custom fusion | bytes 516 | tf_op jit(solution)/shard_map/scatter | solution.py:46
  3.6 0.7 %all_to_all.9 = f32[8,1,16]{2,0,1:T(8,128)} reshape(f32[128]{0:T(128)S(1)} %scatter_custom_fusion) | data formatting | bytes 1024 | tf_op jit(solution)/shard_map/all_to_all | solution.py:56
  4.3 5.2 %all-to-all-start = ((f32[8,1,16]{2,1,0:T(1,128)}), f32[8,1,16]{2,1,0:T(1,128)S(1)}, u32[]{:S(2)}, u32[]{:S(2)}) async-start(f32[8,1,16]{2,1,0:T(1,128)} %bitcast.4), calls=%async_computation | async-start | bytes 8192 | tf_op jit(solution)/shard_map/all_to_all | solution.py:56
  9.5 1.9 %reduce_sum.74 = f32[32,3,512]{2,1,0:T(4,128)S(1)} reduce(f32[32,3,8,512]{3,2,1,0:T(8,128)} %param.6, f32[]{:T(128)} %constant.11.clone.1), dimensions={2}, to_apply=%region_4.5 | reduce | flops 344064 | bytes 1769476 | tf_op jit(solution)/shard_map/reduce_sum | solution.py:33
  11.3 0.0 copy-start
  11.3 0.1 broadcast_multiply_fusion
  11.4 0.1 copy.32
  11.5 1.6 %scatter_custom_fusion.2 = f32[128,1536]{1,0:T(8,128)} fusion(s32[32]{0:T(128)S(1)} %get-tuple-element.14, f32[32,1536]{1,0:T(8,128)S(1)} %bitcast.31, f32[]{:T(128)} %constant.11.clone.1), kind=kCustom, calls=%fused_computation.15 | custom fusion | bytes 786436 | tf_op jit(solution)/shard_map/scatter | solution.py:42
  13.1 1.0 %all-to-all-done = f32[8,1,16]{2,1,0:T(1,128)S(1)} async-done(((f32[8,1,16]{2,1,0:T(1,128)}), f32[8,1,16]{2,1,0:T(1,128)S(1)}, u32[]{:S(2)}, u32[]{:S(2)}) %all-to-all-start) | async-done | bytes 544 | tf_op jit(solution)/shard_map/all_to_all | solution.py:56
  14.0 4.2 %all-to-all-start.1 = ((f32[8,16,1536]{2,1,0:T(8,128)}), f32[8,16,1536]{2,1,0:T(8,128)}, u32[]{:S(2)}, u32[]{:S(2)}) async-start(f32[8,16,1536]{2,1,0:T(8,128)} %bitcast.6), calls=%async_computation.1 | async-start | bytes 1572864 | tf_op jit(solution)/shard_map/all_to_all | solution.py:49
  18.3 0.0 copy-done
  18.3 0.0 copy-start.1
  18.3 0.3 copy.25
  18.5 0.3 copy.26
  18.8 0.4 copy-done.1
  19.2 0.1 copy.28
  19.4 0.1 sub.20
  19.5 1.0 %scatter_custom_fusion.1 = f32[128]{0:T(128)S(1)} fusion(s32[128]{0:T(128)S(1)} %fusion.10, f32[128]{0:T(128)S(1)} %broadcast.88, f32[]{:T(128)} %constant.11.clone.1), kind=kCustom, calls=%fused_computation.38 | custom fusion | bytes 516 | tf_op jit(solution)/shard_map/scatter | solution.py:67
  20.5 10.4 %all-to-all-done.1 = f32[8,16,1536]{2,1,0:T(8,128)} async-done(((f32[8,16,1536]{2,1,0:T(8,128)}), f32[8,16,1536]{2,1,0:T(8,128)}, u32[]{:S(2)}, u32[]{:S(2)}) %all-to-all-start.1) | async-done | bytes 786464 | tf_op jit(solution)/shard_map/all_to_all | solution.py:49
  30.9 1.9 %scatter_custom_fusion.3 = f32[128,1536]{1,0:T(8,128)S(1)} fusion(s32[128]{0:T(128)S(1)} %fusion.10, f32[128,1536]{1,0:T(8,128)} %bitcast.7, f32[]{:T(128)} %constant.11.clone.1), kind=kCustom, calls=%fused_computation.13 | custom fusion | bytes 786944 | tf_op jit(solution)/shard_map/scatter | solution.py:65
  32.8 0.1 broadcast_select_fusion
  32.9 0.3 copy.27
  33.2 0.1 fusion
  33.3 0.1 fusion.1
  33.4 0.1 fusion.2
  33.4 0.1 multiply_reduce_fusion
  33.6 0.1 multiply_reduce_fusion.3
  33.7 0.1 copy.30
  33.8 0.1 reshape.78
  33.9 0.1 fusion.7
  34.1 0.1 reduce_sum.80
  34.2 12.1 %all-reduce.3 = (f32[8]{0:T(128)S(1)}, f32[1024]{0:T(1024)S(1)}) all-reduce(f32[8]{0:T(128)S(1)} %reduce_sum.81, f32[1024]{0:T(1024)S(1)} %reshape.78), channel_id=1, replica_groups=mesh['blk'=8,'sig'=4] {'sig'}, use_global_device_ids=true, to_apply=%region_14.15 | all-reduce | flops 1032 | bytes 8256 | tf_op jit(solution)/shard_map/psum | solution.py:75
  46.3 0.6 %broadcast_in_dim.27 = f32[1,1032]{1,0:T(1,128)} reshape(f32[1032]{0:T(1024)S(1)} %pad_maximum_fusion) | data formatting | bytes 8256 | tf_op jit(solution)/shard_map/broadcast_in_dim | solution.py:78
  46.9 1.1 %copy.31 = f32[128,3,512]{2,0,1:T(8,128)} copy(f32[128,3,512]{0,2,1:T(8,128)S(1)} %bitcast.27) | data formatting | bytes 1572864
  (11 shorter events, 0.2 us)
Async XLA Ops:
  4.3 9.8 %all-to-all-start = ((f32[8,1,16]{2,1,0:T(1,128)}), f32[8,1,16]{2,1,0:T(1,128)S(1)}, u32[]{:S(2)}, u32[]{:S(2)}) async-start(f32[8,1,16]{2,1,0:T(1,128)} %bitcast.4), calls=%async_computation | async-start | bytes 8192 | tf_op jit(solution)/shard_map/all_to_all | solution.py:56
  11.3 6.9 %copy-start = (f32[128,3,512]{2,0,1:T(8,128)S(1)}, f32[128,3,512]{2,0,1:T(8,128)}, u32[]{:S(2)}) copy-start(f32[128,3,512]{2,0,1:T(8,128)} %param.5) | copy-start | bytes 2359300
  14.0 16.8 %all-to-all-start.1 = ((f32[8,16,1536]{2,1,0:T(8,128)}), f32[8,16,1536]{2,1,0:T(8,128)}, u32[]{:S(2)}, u32[]{:S(2)}) async-start(f32[8,16,1536]{2,1,0:T(8,128)} %bitcast.6), calls=%async_computation.1 | async-start | bytes 1572864 | tf_op jit(solution)/shard_map/all_to_all | solution.py:49
  18.3 1.0 %copy-start.1 = (s32[128,512]{1,0:T(8,128)S(1)}, s32[128,512]{1,0:T(8,128)}, u32[]{:S(2)}) copy-start(s32[128,512]{1,0:T(8,128)} %param.9) | copy-start | bytes 786436
where the time goes:
time: 48.5 us; the launch traced here: 48.1 us
  blocking collectives  12.1 us (25%)
  waiting for transfers between devices  11.3 us (23%)
  starting transfers between devices  9.37 us (19%)
  local copies, waits for them, and re-layouts  9.3 us (19%)
  other arithmetic  5.11 us (11%)
  between operations  0.86 us (2%)
    psum x1, blocking collectives, shards(): sum_y, sum_z = lax.psum((part_y, part_z), 'sig')  12.1 us
    all_to_all x1, waiting for transfers between devices, shards(): lax.all_to_all(send_data.reshape(blocks, capacity, width), 'blk', split_a...  10.4 us
    all_to_all x1, starting transfers between devices, shards(): lax.all_to_all(send_tiles.reshape(blocks, capacity), 'blk', split_axis=0,...  5.17 us
    all_to_all x1, starting transfers between devices, shards(): lax.all_to_all(send_data.reshape(blocks, capacity, width), 'blk', split_a...  4.2 us
    unnamed x8, local copies, waits for them, and re-layouts  2 us
    scatter x1, local copies, waits for them, and re-layouts, shards(): totals = jnp.zeros((tile_count, width), jnp.float32).at[tile_of_slot].set...  1.89 us
    reduce_sum x1, other arithmetic, shards(): child_mean = 0.125 * jnp.sum(fine_fields, axis=2)  1.86 us
    scatter x1, local copies, waits for them, and re-layouts, shards(): jnp.zeros((blocks * capacity, width), jnp.float32).at[slot_index]  1.61 us
  transfers between devices with their start and end apart: 2, of which 2 were waited for; matrix products, arithmetic and copies ran while one was open for 11% of the time, Pallas kernels for 0%

commit v1 on v0

v1 whole, which is shorter than its diff:
```python
import functools

import jax
import jax.numpy as jnp
from jax import lax
from jax.experimental import pallas as pl
from jax.experimental.pallas import tpu as pltpu
from jax.sharding import PartitionSpec as P

EDGE = 8
FIELDS = 3
MESH = pl.DeviceIdType.MESH


def plan(blocks):
    if blocks == 8:
        steps = {
            "x0": (0, 0, 1, 2, 2, None),
            "y1": (0, 1, 1, 4, 4, None),
            "x1": (0, 1, 1, 2, 2, None),
            "y0": (0, 0, 1, 4, 4, None),
            "c": (0, 0, 2, 1, 1, None),
            "d0": (2, 0, 1, 4, 6, "x0"),
            "d1": (4, 1, 1, 2, 6, "y1"),
            "cx0": (2, 0, 1, 1, 3, "x0"),
            "cy1": (4, 1, 1, 1, 5, "y1"),
            "cx1": (2, 1, 1, 1, 3, "x1"),
            "cy0": (4, 0, 1, 1, 5, "y0"),
            "cd0": (6, 0, 1, 1, 7, "d0"),
            "cd1": (6, 1, 1, 1, 7, "d1"),
        }
        return steps
    return None


def kernel(
    blocks, slabs,
    coarse_hbm, fine_hbm, owner_hbm, target_hbm, tags_hbm,
    synced_ref, sig_ref,
    fine, coarse, tags, own_i, tgt_i, meta, rec, turned, tags_t, parts,
    load_sem, msend, mrecv, dsend, drecv, ssend, srecv,
):
    tile_count = coarse.shape[1]
    cells = coarse.shape[2]
    patches = fine.shape[0]
    half = patches // 2
    me = lax.axis_index("blk")
    slab = lax.axis_index("sig")

    def partner(mask):
        index = me
        bit = 1
        while bit <= mask:
            if mask & bit:
                index = index + bit - 2 * bit * ((me // bit) % 2)
            bit *= 2
        return index

    def load(k, src, dst):
        copy = pltpu.make_async_copy(src, dst, load_sem.at[k])
        copy.start()
        return copy

    load_owner = load(0, owner_hbm, own_i)
    load_target = load(1, target_hbm, tgt_i)
    load_fine = [
        load(2 + h, fine_hbm.at[pl.ds(h * half, half)], fine.at[pl.ds(h * half, half)]) for h in range(2)
    ]
    load_tags = load(4, tags_hbm, tags)
    load_coarse = load(5, coarse_hbm, coarse)

    barrier = pltpu.get_barrier_semaphore()
    for mask in range(1, blocks):
        pl.semaphore_signal(barrier, inc=1, device_id={"blk": partner(mask)}, device_id_type=MESH)
    for shift in range(1, slabs):
        pl.semaphore_signal(
            barrier, inc=1, device_id={"sig": lax.rem(slab + shift, slabs)}, device_id_type=MESH
        )

    load_owner.wait()
    load_target.wait()
    code = own_i[...] * tile_count + tgt_i[...]
    wide = jnp.concatenate([code] * (128 // patches), axis=1).astype(jnp.float32)
    meta[0] = jnp.broadcast_to(wide, (8, 128))

    def average(h):
        load_fine[h].wait()
        for f in range(FIELDS):
            rec[0, h, f] = 0.125 * jnp.sum(fine[h * half : (h + 1) * half, f], axis=1)

    average(0)
    pl.semaphore_wait(barrier, blocks - 1 + slabs - 1)

    started = []

    def send(src, dst, send_sem, recv_sem, device):
        copy = pltpu.make_async_remote_copy(
            src_ref=src, dst_ref=dst, send_sem=send_sem, recv_sem=recv_sem,
            device_id=device, device_id_type=MESH,
        )
        copy.start()
        started.append(copy)
        return copy

    def split(x):
        high = x.astype(jnp.bfloat16)
        low = (x - high.astype(jnp.float32)).astype(jnp.bfloat16)
        return jnp.concatenate([high, low], axis=0)

    lane = lax.broadcasted_iota(jnp.int32, (tile_count, 4 * patches), 1)
    first = (lane // patches) % 2 == 0
    tile_codes = (
        lax.broadcasted_iota(jnp.int32, (tile_count, 4 * patches), 0) + me * tile_count
    ).astype(jnp.float32)

    def place(group):
        codes = jnp.where(first, meta[2 * group][0:1], meta[2 * group + 1][0:1])
        return jnp.where(codes == tile_codes, 1.0, 0.0).astype(jnp.float32)

    def add(group):
        chosen = place(group).astype(jnp.bfloat16)
        for f in range(FIELDS):
            rows = rec[pl.ds(2 * group, 2), :, f].reshape(2 * patches, cells)
            synced_ref[f] += jnp.dot(chosen, split(rows), preferred_element_type=jnp.float32)

    def prepare():
        load_tags.wait()
        tags_t[...] = (0.25 * tags[...].astype(jnp.float32)).T.reshape(tags_t.shape)
        for copy in metas:
            copy.wait_recv()
        if blocks <= 8:
            hits = place(0)
            for group in range(1, blocks // 2):
                hits = hits + place(group)
        else:
            hits = lax.fori_loop(
                0, blocks // 2, lambda group, total: total + place(group),
                jnp.zeros((tile_count, 4 * patches), jnp.float32),
            )
        free = jnp.max(hits, axis=1, keepdims=True) == 0
        load_coarse.wait()
        for f in range(FIELDS):
            synced_ref[f] = jnp.where(free, coarse[f], 0.0)

    steps = plan(blocks)
    metas = []

    def send_metas():
        for mask in range(1, blocks):
            metas.append(
                send(meta.at[0], meta.at[mask], msend.at[mask], mrecv.at[mask], {"blk": partner(mask)})
            )

    if steps is not None:
        names = list(steps)
        copies = {}

        def go(name):
            slot, start, count, mask, target, _ = steps[name]
            k = names.index(name)
            copies[name] = send(
                rec.at[slot, pl.ds(start, count)], rec.at[target, pl.ds(start, count)],
                dsend.at[k], drecv.at[k], {"blk": partner(mask)},
            )

        go("x0")
        go("y0")
        send_metas()
        average(1)
        go("y1")
        go("x1")
        go("c")
        prepare()
        copies["x0"].wait_recv()
        go("d0")
        go("cx0")
        copies["y1"].wait_recv()
        go("d1")
        go("cy1")
        copies["c"].wait_recv()
        add(0)
        copies["y0"].wait_recv()
        go("cy0")
        copies["x1"].wait_recv()
        go("cx1")
        copies["cx0"].wait_recv()
        copies["cx1"].wait_recv()
        add(1)
        copies["cy0"].wait_recv()
        copies["cy1"].wait_recv()
        add(2)
        copies["d0"].wait_recv()
        go("cd0")
        copies["d1"].wait_recv()
        go("cd1")
        copies["cd0"].wait_recv()
        copies["cd1"].wait_recv()
        add(3)
    else:
        send_metas()
        average(1)
        bit, k = 1, 0
        while bit < blocks:
            send(
                rec.at[pl.ds(0, bit)], rec.at[pl.ds(bit, bit)], dsend.at[k], drecv.at[k], {"blk": partner(bit)}
            ).wait_recv()
            bit, k = 2 * bit, k + 1
        prepare()

        def body(group, carry):
            add(group)
            return carry

        lax.fori_loop(0, blocks // 2, body, 0)

    for f in range(FIELDS):
        turned[f] = synced_ref[f].T.reshape(turned.shape[1:])

    depth = lax.broadcasted_iota(jnp.int32, (EDGE, EDGE, tile_count), 1)
    inner_z = (depth > 0) & (depth < EDGE - 1)
    total = jnp.zeros((EDGE, EDGE, tile_count), jnp.float32)
    edge_row = jnp.zeros((1, EDGE, tile_count), jnp.float32)
    for x in range(EDGE):
        sum_x = sum_y = sum_z = None
        for f in range(FIELDS):
            mid = turned[f, x]
            dy = mid[2:] - mid[:-2]
            dz = mid - pltpu.roll(mid, 2, 1)
            sum_y = dy * dy if f == 0 else sum_y + dy * dy
            sum_z = dz * dz if f == 0 else sum_z + dz * dz
            if 0 < x < EDGE - 1:
                dx = turned[f, x + 1] - turned[f, x - 1]
                sum_x = dx * dx if f == 0 else sum_x + dx * dx
        value = jnp.where(inner_z, pltpu.roll(sum_z, EDGE - 1, 1), 0.0)
        value = value + jnp.concatenate([edge_row, sum_y, edge_row], axis=0)
        if sum_x is not None:
            value = value + sum_x
        total = total + tags_t[x] * value

    parts[slab, 0] = jnp.sum(total, axis=1)
    parts[slab, 1] = jnp.sum(total, axis=0)
    sums = []
    for shift in range(1, slabs):
        sums.append(
            send(
                parts.at[slab], parts.at[slab], ssend.at[shift], srecv.at[shift],
                {"sig": lax.rem(slab + shift, slabs)},
            )
        )
    for shift in range(1, slabs):
        came = lax.rem(slab + slabs - shift, slabs)
        pltpu.make_async_remote_copy(
            src_ref=parts.at[came], dst_ref=parts.at[came], send_sem=ssend.at[shift], recv_sem=srecv.at[shift],
            device_id={"sig": lax.rem(slab + shift, slabs)}, device_id_type=MESH,
        ).wait_recv()
    whole = parts[0]
    for k in range(1, slabs):
        whole = whole + parts[k]

    along_y = whole[0] * (1.0 / (EDGE * EDGE * slabs))
    along_z = whole[1] * (1.0 / (EDGE * EDGE * tile_count * slabs))
    group = 128 // EDGE
    spread = jnp.concatenate([along_y] * group, axis=0)
    row = lax.broadcasted_iota(jnp.int32, (128, tile_count), 0)
    col = lax.broadcasted_iota(jnp.int32, (128, tile_count), 1)
    spread = jnp.where(col % group == row // EDGE, spread, 0.0)
    lines = tile_count // group
    pick = (
        lax.broadcasted_iota(jnp.int32, (lines, tile_count), 1) // group
        == lax.broadcasted_iota(jnp.int32, (lines, tile_count), 0)
    ).astype(jnp.float32)
    across = (((1,), (1,)), ((), ()))
    order = lax.dot_general(
        pick, spread, across, precision=lax.Precision.HIGHEST, preferred_element_type=jnp.float32
    )
    last = lax.dot_general(
        jnp.ones((8, tile_count), jnp.float32), along_z, across,
        precision=lax.Precision.HIGHEST, preferred_element_type=jnp.float32,
    )
    for r in range(lines):
        sig_ref[0:1, r * 128 : (r + 1) * 128] = order[r : r + 1]
    sig_ref[0:1, lines * 128 : lines * 128 + EDGE] = last[0:1]

    for copy in started:
        copy.wait_send()


def shards(blocks, slabs, coarse_fields, fine_fields, owner, target_tile, tags):
    tile_count, _, cells = coarse_fields.shape
    patches = fine_fields.shape[0]
    coarse = jnp.transpose(coarse_fields, (1, 0, 2))
    anywhere = pl.BlockSpec(memory_space=pl.ANY)
    vmem = pl.BlockSpec(memory_space=pltpu.VMEM)
    copies = 16
    f32 = jnp.float32
    synced, signature = pl.pallas_call(
        functools.partial(kernel, blocks, slabs),
        out_shape=(
            jax.ShapeDtypeStruct((FIELDS, tile_count, cells), f32),
            jax.ShapeDtypeStruct((1, tile_count * EDGE + EDGE), f32),
        ),
        in_specs=[anywhere] * 5,
        out_specs=(vmem, vmem),
        scratch_shapes=[
            pltpu.VMEM(fine_fields.shape, f32),
            pltpu.VMEM((FIELDS, tile_count, cells), f32),
            pltpu.VMEM((tile_count, cells), jnp.int32),
            pltpu.VMEM((1, patches), jnp.int32),
            pltpu.VMEM((1, patches), jnp.int32),
            pltpu.VMEM((blocks, 8, 128), f32),
            pltpu.VMEM((blocks, 2, FIELDS, patches // 2, cells), f32),
            pltpu.VMEM((FIELDS, EDGE, EDGE, EDGE, tile_count), f32),
            pltpu.VMEM((EDGE, EDGE, EDGE, tile_count), f32),
            pltpu.VMEM((slabs, 2, EDGE, tile_count), f32),
            pltpu.SemaphoreType.DMA((6,)),
            pltpu.SemaphoreType.DMA((blocks,)),
            pltpu.SemaphoreType.DMA((blocks,)),
            pltpu.SemaphoreType.DMA((copies,)),
            pltpu.SemaphoreType.DMA((copies,)),
            pltpu.SemaphoreType.DMA((slabs,)),
            pltpu.SemaphoreType.DMA((slabs,)),
        ],
        compiler_params=pltpu.CompilerParams(
            collective_id=0, has_side_effects=True, vmem_limit_bytes=32 * 1024 * 1024
        ),
        name="average_down",
    )(coarse, fine_fields, owner.reshape(1, patches), target_tile.reshape(1, patches), tags)
    return jnp.transpose(synced, (1, 0, 2)), signature


def solution(mesh):
    blocks, slabs = mesh.shape["blk"], mesh.shape["sig"]
    return jax.shard_map(
        functools.partial(shards, blocks, slabs),
        mesh=mesh,
        in_specs=(
            P(("blk", "sig"), None, None),
            P(("blk", "sig"), None, None, None),
            P(("blk", "sig"), None),
            P(("blk", "sig"), None),
            P(("blk", "sig"), None),
        ),
        out_specs=(P(("blk", "sig"), None, None), P("blk", None)),
        check_vma=False,
    )
```

time: 48.5 us -> 27.8 us (0.57)
  Pallas kernels: 0 us -> 20.6 us
  blocking collectives: 12.1 us -> 0 us
  waiting for transfers between devices: 11.3 us -> 0 us
  starting transfers between devices: 9.37 us -> 0 us
  other arithmetic: 5.11 us -> 0 us
  local copies, waits for them, and re-layouts: 9.3 us -> 6.27 us
    pallas_call x0 -> x1, Pallas kernels: none -> 20.6 us  [shards(): pl.pallas_call(functools.partial(kernel, blocks, slabs), out_shape=(jax.S...]
    psum x1 -> x0, blocking collectives: 12.1 us -> none  [shards(): sum_y, sum_z = lax.psum((part_y, part_z), 'sig')]
    all_to_all x2 -> x0, waiting for transfers between devices: 11.3 us -> none  [the longest x1 10.4 us: shards(): lax.all_to_all(send_data.reshape(blocks, capacity, width), 'blk', split_a...]
    all_to_all x2 -> x0, starting transfers between devices: 9.37 us -> none  [the longest x1 5.17 us: shards(): lax.all_to_all(send_tiles.reshape(blocks, capacity), 'blk', split_axis=0,...]
    scatter x4 -> x0, local copies, waits for them, and re-layouts: 5.14 us -> none  [the longest x1 1.89 us: shards(): totals = jnp.zeros((tile_count, width), jnp.float32).at[tile_of_slot].set...]
    unnamed x8 -> x12, local copies, waits for them, and re-layouts: 2 us -> 6.27 us
    reduce_sum x8 -> x0, other arithmetic: 3.15 us -> none  [the longest x1 1.86 us: shards(): child_mean = 0.125 * jnp.sum(fine_fields, axis=2)]
    select_n x3 -> x0, other arithmetic: 0.83 us -> none  [the longest x1 0.68 us: shards(): send_tiles = jnp.zeros((blocks * capacity,), jnp.float32).at[slot_index]....]
  transfers between devices with their start and end apart: 2 -> 0, of which waited for: 2 -> 0; matrix products, arithmetic and copies ran while one was open for 11% -> 0% of each run, Pallas kernels for 0% -> 0%
where the time goes in v1:
time: 27.8 us; the launch traced here: 27.6 us
  Pallas kernels  20.6 us (74%)
  local copies, waits for them, and re-layouts  6.27 us (23%)
  between operations  0.65 us (2%)
    pallas_call x1, Pallas kernels, shards(): pl.pallas_call(functools.partial(kernel, blocks, slabs), out_shape=(jax.S...  20.6 us
    unnamed x12, local copies, waits for them, and re-layouts  6.27 us

profile of v1, /device:TPU:0, one launch (start us, length us, event | category | flops | bytes accessed | tf_op | source)
XLA Modules:
  0.0 27.6 jit_solution(17252009130089734732)
XLA Ops:
  0.6 0.0 copy-start
  0.6 1.4 %copy-done = f32[32,3,8,512]{3,2,1,0:T(8,128)S(1)} copy-done((f32[32,3,8,512]{3,2,1,0:T(8,128)S(1)}, f32[32,3,8,512]{3,2,1,0:T(8,128)}, u32[]{:S(2)}) %copy-start) | copy-done | bytes 1572888
  2.0 0.0 copy-start.1
  2.0 1.1 %copy-done.1 = f32[128,3,512]{2,0,1:T(8,128)S(1)} copy-done((f32[128,3,512]{2,0,1:T(8,128)S(1)}, f32[128,3,512]{2,0,1:T(8,128)}, u32[]{:S(2)}) %copy-start.1) | copy-done | bytes 786456
  3.2 0.0 copy-start.2
  3.2 0.9 %copy-done.2 = s32[128,512]{1,0:T(8,128)S(1)} copy-done((s32[128,512]{1,0:T(8,128)S(1)}, s32[128,512]{1,0:T(8,128)}, u32[]{:S(2)}) %copy-start.2) | copy-done | bytes 262168
  4.1 0.0 copy-start.3
  4.1 0.7 %copy-done.3 = s32[32,1]{0,1:T(1,128)S(1)} copy-done((s32[32,1]{0,1:T(1,128)S(1)}, s32[32,1]{0,1:T(1,128)}, u32[]{:S(2)}) %copy-start.3) | copy-done | bytes 152
  4.8 0.0 copy-start.4
  4.8 0.7 %copy-done.4 = s32[32,1]{0,1:T(1,128)S(1)} copy-done((s32[32,1]{0,1:T(1,128)S(1)}, s32[32,1]{0,1:T(1,128)}, u32[]{:S(2)}) %copy-start.4) | copy-done | bytes 152
  5.4 20.6 %average_down.1 = (f32[3,128,512]{2,1,0:T(8,128)S(1)}, f32[1,1032]{1,0:T(1,128)S(1)}) custom-call(f32[3,128,512]{2,1,0:T(8,128)S(1)} %bitcast.5, f32[32,3,8,512]{3,2,1,0:T(8,128)S(1)} %copy-done, s32[1,32]{1,0:T(1,128)S(1)} %bitcast.6, s32[1,32]{1,0:T(1,128)S(1)} %bitcast.7, s32[128,512]{1,0:T(8,128)S(1)} %copy-done.2), custom_call_target="tpu_custom_call" | custom-call | tf_op jit(solution)/shard_map/average_down/pallas_call | solution.py:296
  26.1 0.9 %copy.9 = f32[128,3,512]{2,0,1:T(8,128)} copy(f32[128,3,512]{2,0,1:T(8,128)S(1)} %bitcast.4) | data formatting | bytes 1572864
  27.0 0.6 %copy.10 = f32[1,1032]{1,0:T(1,128)} copy(f32[1,1032]{1,0:T(1,128)S(1)} %get-tuple-element.9) | data formatting | bytes 8256
Async XLA Ops:
  0.6 1.4 %copy-start = (f32[32,3,8,512]{3,2,1,0:T(8,128)S(1)}, f32[32,3,8,512]{3,2,1,0:T(8,128)}, u32[]{:S(2)}) copy-start(f32[32,3,8,512]{3,2,1,0:T(8,128)} %fine_hbm.1) | copy-start | bytes 4718596
  2.0 1.1 %copy-start.1 = (f32[128,3,512]{2,0,1:T(8,128)S(1)}, f32[128,3,512]{2,0,1:T(8,128)}, u32[]{:S(2)}) copy-start(f32[128,3,512]{2,0,1:T(8,128)} %param.5) | copy-start | bytes 2359300
  3.2 0.9 %copy-start.2 = (s32[128,512]{1,0:T(8,128)S(1)}, s32[128,512]{1,0:T(8,128)}, u32[]{:S(2)}) copy-start(s32[128,512]{1,0:T(8,128)} %tags_hbm.1) | copy-start | bytes 786436
  4.1 0.7 %copy-start.3 = (s32[32,1]{0,1:T(1,128)S(1)}, s32[32,1]{0,1:T(1,128)}, u32[]{:S(2)}) copy-start(s32[32,1]{0,1:T(1,128)} %param.7) | copy-start | bytes 388
  4.8 0.7 %copy-start.4 = (s32[32,1]{0,1:T(1,128)S(1)}, s32[32,1]{0,1:T(1,128)}, u32[]{:S(2)}) copy-start(s32[32,1]{0,1:T(1,128)} %param.8) | copy-start | bytes 388

commit v2 on v1

v2 whole, which is shorter than its diff:
```python
import functools

import jax
import jax.numpy as jnp
from jax import lax
from jax.experimental import pallas as pl
from jax.experimental.pallas import tpu as pltpu
from jax.sharding import PartitionSpec as P

EDGE = 8
FIELDS = 3
VMEM_BYTES = 62 * 1024 * 1024
MESH = pl.DeviceIdType.MESH


def kernel(
    blocks, slabs,
    coarse_hbm, fine_hbm, owner_hbm, target_hbm, tags_hbm,
    synced_hbm, sums_ref,
    synced_ref, fine, coarse, tags, own_i, tgt_i, meta, rec, turned, tags_t, total, parts,
    load_sem, out_sem, msend, mrecv, dsend, drecv, ssend, srecv,
):
    tile_count = coarse.shape[1]
    cells = coarse.shape[2]
    patches = fine.shape[1]
    me = lax.axis_index("blk")
    slab = lax.axis_index("sig")

    def partner(mask):
        index = me
        bit = 1
        while bit <= mask:
            if mask & bit:
                index = index + bit - 2 * bit * ((me // bit) % 2)
            bit *= 2
        return index

    def load(k, src, dst):
        copy = pltpu.make_async_copy(src, dst, load_sem.at[k])
        copy.start()
        return copy

    load_fine = [load(f, fine_hbm.at[:, f], fine.at[f]) for f in range(FIELDS)]
    load_owner = load(FIELDS, owner_hbm, own_i)
    load_target = load(FIELDS + 1, target_hbm, tgt_i)
    load_tags = load(FIELDS + 2, tags_hbm, tags)
    load_coarse = load(FIELDS + 3, coarse_hbm, coarse)

    barrier = pltpu.get_barrier_semaphore()
    for mask in range(1, blocks):
        pl.semaphore_signal(barrier, inc=1, device_id={"blk": partner(mask)}, device_id_type=MESH)
    for shift in range(1, slabs):
        pl.semaphore_signal(
            barrier, inc=1, device_id={"sig": lax.rem(slab + shift, slabs)}, device_id_type=MESH
        )

    def split(x):
        high = x.astype(jnp.bfloat16)
        return high, (x - high.astype(jnp.float32)).astype(jnp.bfloat16)

    mean = jnp.where(
        lax.broadcasted_iota(jnp.int32, (patches, patches * 8), 1) // 8
        == lax.broadcasted_iota(jnp.int32, (patches, patches * 8), 0),
        0.125, 0.0,
    ).astype(jnp.bfloat16)

    def average(f):
        load_fine[f].wait()
        high, low = split(fine[f].reshape(patches * 8, cells))
        rows = jnp.dot(mean, high, preferred_element_type=jnp.float32)
        rows = rows + jnp.dot(mean, low, preferred_element_type=jnp.float32)
        rec[0, f] = rows.reshape(rec.shape[2:])

    average(0)
    load_owner.wait()
    load_target.wait()
    code = own_i[...] * tile_count + tgt_i[...]
    wide = jnp.concatenate([code] * (128 // patches), axis=1).astype(jnp.float32)
    meta[0] = jnp.broadcast_to(wide, (8, 128))
    pl.semaphore_wait(barrier, blocks - 1 + slabs - 1)

    started = []
    writes = []

    def send(src, dst, send_sem, recv_sem, device):
        copy = pltpu.make_async_remote_copy(
            src_ref=src, dst_ref=dst, send_sem=send_sem, recv_sem=recv_sem,
            device_id=device, device_id_type=MESH,
        )
        copy.start()
        started.append(copy)
        return copy

    lane = lax.broadcasted_iota(jnp.int32, (tile_count, 4 * patches), 1)
    first = (lane // patches) % 2 == 0
    tile_codes = (
        lax.broadcasted_iota(jnp.int32, (tile_count, 4 * patches), 0) + me * tile_count
    ).astype(jnp.float32)

    def place(group):
        codes = jnp.where(first, meta[2 * group][0:1], meta[2 * group + 1][0:1])
        return jnp.where(codes == tile_codes, 1.0, 0.0).astype(jnp.float32)

    def add(group, f):
        rows = rec[pl.ds(2 * group, 2), f].reshape(2 * patches, cells)
        synced_ref[f] += jnp.dot(
            place(group).astype(jnp.bfloat16), jnp.concatenate(split(rows), axis=0),
            preferred_element_type=jnp.float32,
        )

    def prepare():
        load_tags.wait()
        tags_t[...] = (0.25 * tags[...].astype(jnp.float32)).T.reshape(tags_t.shape)
        total[...] = jnp.zeros_like(total)
        for copy in metas:
            copy.wait_recv()
        if blocks <= 8:
            hits = place(0)
            for group in range(1, blocks // 2):
                hits = hits + place(group)
        else:
            hits = lax.fori_loop(
                0, blocks // 2, lambda group, found: found + place(group),
                jnp.zeros((tile_count, 4 * patches), jnp.float32),
            )
        free = jnp.max(hits, axis=1, keepdims=True) == 0
        load_coarse.wait()
        for f in range(FIELDS):
            synced_ref[f] = jnp.where(free, coarse[f], 0.0)

    depth = lax.broadcasted_iota(jnp.int32, (EDGE, EDGE, tile_count), 1)
    inner_z = (depth > 0) & (depth < EDGE - 1)
    edge_row = jnp.zeros((1, EDGE, tile_count), jnp.float32)

    def weigh(f):
        writes.append(pltpu.make_async_copy(synced_ref.at[f], synced_hbm.at[f], out_sem.at[f]))
        writes[-1].start()
        turned[...] = synced_ref[f].T.reshape(turned.shape)
        for x in range(EDGE):
            mid = turned[x]
            dy = mid[2:] - mid[:-2]
            dz = mid - pltpu.roll(mid, 2, 1)
            value = jnp.where(inner_z, pltpu.roll(dz * dz, EDGE - 1, 1), 0.0)
            value = value + jnp.concatenate([edge_row, dy * dy, edge_row], axis=0)
            if 0 < x < EDGE - 1:
                dx = turned[x + 1] - turned[x - 1]
                value = value + dx * dx
            total[...] += tags_t[x] * value

    metas = []

    def send_metas():
        for mask in range(1, blocks):
            metas.append(
                send(meta.at[0], meta.at[mask], msend.at[mask], mrecv.at[mask], {"blk": partner(mask)})
            )

    if blocks == 8:
        copies = {}

        def go(name, slot, start, count, mask, target, f):
            k = len(copies)
            copies[name, f] = send(
                rec.at[slot, f, pl.ds(start, count)], rec.at[target, f, pl.ds(start, count)],
                dsend.at[k], drecv.at[k], {"blk": partner(mask)},
            )

        def came(f, *names):
            for name in names:
                copies[name, f].wait_recv()

        def own(f):
            go("x0", 0, 0, 1, 2, 2, f)
            go("y1", 0, 1, 1, 4, 4, f)
            go("x1", 0, 1, 1, 2, 2, f)
            go("y0", 0, 0, 1, 4, 4, f)
            go("c", 0, 0, 2, 1, 1, f)

        def forward(f):
            came(f, "x0")
            go("d0", 2, 0, 1, 4, 6, f)
            go("cx0", 2, 0, 1, 1, 3, f)
            came(f, "y1")
            go("d1", 4, 1, 1, 2, 6, f)
            go("cy1", 4, 1, 1, 1, 5, f)

        def share(f):
            came(f, "x1")
            go("cx1", 2, 1, 1, 1, 3, f)
            came(f, "y0")
            go("cy0", 4, 0, 1, 1, 5, f)

        def share_diagonal(f):
            came(f, "d0")
            go("cd0", 6, 0, 1, 1, 7, f)
            came(f, "d1")
            go("cd1", 6, 1, 1, 1, 7, f)

        def add_near(f):
            came(f, "c")
            add(0, f)
            came(f, "cx0", "cx1")
            add(1, f)
            came(f, "cy0", "cy1")
            add(2, f)

        def add_diagonal(f):
            came(f, "cd0", "cd1")
            add(3, f)

        own(0)
        send_metas()
        average(1)
        own(1)
        average(2)
        prepare()
        forward(0)
        own(2)
        share(0)
        forward(1)
        add_near(0)
        share(1)
        share_diagonal(0)
        forward(2)
        add_near(1)
        share(2)
        add_diagonal(0)
        weigh(0)
        share_diagonal(1)
        add_near(2)
        share_diagonal(2)
        add_diagonal(1)
        weigh(1)
        add_diagonal(2)
        weigh(2)
    else:
        send_metas()
        average(1)
        average(2)
        bit, k = 1, 0
        while bit < blocks:
            send(
                rec.at[pl.ds(0, bit)], rec.at[pl.ds(bit, bit)], dsend.at[k], drecv.at[k], {"blk": partner(bit)}
            ).wait_recv()
            bit, k = 2 * bit, k + 1
        prepare()

        def body(group, carry):
            for f in range(FIELDS):
                add(group, f)
            return carry

        lax.fori_loop(0, blocks // 2, body, 0)
        for f in range(FIELDS):
            weigh(f)

    parts[slab, 0] = jnp.sum(total[...], axis=1)
    parts[slab, 1] = jnp.sum(total[...], axis=0)
    for shift in range(1, slabs):
        send(
            parts.at[slab], parts.at[slab], ssend.at[shift], srecv.at[shift],
            {"sig": lax.rem(slab + shift, slabs)},
        )
    for shift in range(1, slabs):
        source = lax.rem(slab + slabs - shift, slabs)
        pltpu.make_async_remote_copy(
            src_ref=parts.at[source], dst_ref=parts.at[source], send_sem=ssend.at[shift], recv_sem=srecv.at[shift],
            device_id={"sig": lax.rem(slab + shift, slabs)}, device_id_type=MESH,
        ).wait_recv()
    whole = parts[0]
    for k in range(1, slabs):
        whole = whole + parts[k]
    sums_ref[...] = whole

    for copy in started:
        copy.wait_send()
    for copy in writes:
        copy.wait()


def finish(slabs, synced_in, sums, synced_out, signature, line, sem):
    write = pltpu.make_async_copy(synced_in, synced_out, sem.at[0])
    write.start()
    tile_count = sums.shape[2]
    along_y = sums[0] * (1.0 / (EDGE * EDGE * slabs))
    along_z = sums[1] * (1.0 / (EDGE * EDGE * tile_count * slabs))
    group = 128 // EDGE
    spread = jnp.concatenate([along_y] * group, axis=0)
    row = lax.broadcasted_iota(jnp.int32, (128, tile_count), 0)
    col = lax.broadcasted_iota(jnp.int32, (128, tile_count), 1)
    spread = jnp.where(col % group == row // EDGE, spread, 0.0)
    lines = tile_count // group
    pick = (
        lax.broadcasted_iota(jnp.int32, (lines, tile_count), 1) // group
        == lax.broadcasted_iota(jnp.int32, (lines, tile_count), 0)
    ).astype(jnp.float32)
    across = (((1,), (1,)), ((), ()))
    order = lax.dot_general(
        pick, spread, across, precision=lax.Precision.HIGHEST, preferred_element_type=jnp.float32
    )
    last = lax.dot_general(
        jnp.ones((8, tile_count), jnp.float32), along_z, across,
        precision=lax.Precision.HIGHEST, preferred_element_type=jnp.float32,
    )
    for r in range(lines):
        line[0:1, r * 128 : (r + 1) * 128] = order[r : r + 1]
    line[0:1, lines * 128 : lines * 128 + EDGE] = last[0:1]
    write_line = pltpu.make_async_copy(line, signature, sem.at[1])
    write_line.start()
    write_line.wait()
    write.wait()


def shards(blocks, slabs, coarse_fields, fine_fields, owner, target_tile, tags):
    tile_count, _, cells = coarse_fields.shape
    patches = fine_fields.shape[0]
    coarse = jnp.transpose(coarse_fields, (1, 0, 2))
    stay = pl.BlockSpec(memory_space=pl.ANY)
    vmem = pl.BlockSpec(memory_space=pltpu.VMEM)
    copies = 13 * FIELDS
    f32 = jnp.float32
    synced, sums = pl.pallas_call(
        functools.partial(kernel, blocks, slabs),
        out_shape=(
            jax.ShapeDtypeStruct((FIELDS, tile_count, cells), f32),
            jax.ShapeDtypeStruct((2, EDGE, tile_count), f32),
        ),
        in_specs=[stay] * 5,
        out_specs=(stay, vmem),
        scratch_shapes=[
            pltpu.VMEM((FIELDS, tile_count, cells), f32),
            pltpu.VMEM((FIELDS, patches, 8, cells), f32),
            pltpu.VMEM((FIELDS, tile_count, cells), f32),
            pltpu.VMEM((tile_count, cells), jnp.int32),
            pltpu.VMEM((1, patches), jnp.int32),
            pltpu.VMEM((1, patches), jnp.int32),
            pltpu.VMEM((blocks, 8, 128), f32),
            pltpu.VMEM((blocks, FIELDS, 2, patches // 2, cells), f32),
            pltpu.VMEM((EDGE, EDGE, EDGE, tile_count), f32),
            pltpu.VMEM((EDGE, EDGE, EDGE, tile_count), f32),
            pltpu.VMEM((EDGE, EDGE, tile_count), f32),
            pltpu.VMEM((slabs, 2, EDGE, tile_count), f32),
            pltpu.SemaphoreType.DMA((FIELDS + 4,)),
            pltpu.SemaphoreType.DMA((FIELDS,)),
            pltpu.SemaphoreType.DMA((blocks,)),
            pltpu.SemaphoreType.DMA((blocks,)),
            pltpu.SemaphoreType.DMA((copies,)),
            pltpu.SemaphoreType.DMA((copies,)),
            pltpu.SemaphoreType.DMA((slabs,)),
            pltpu.SemaphoreType.DMA((slabs,)),
        ],
        compiler_params=pltpu.CompilerParams(
            collective_id=0, has_side_effects=True, vmem_limit_bytes=VMEM_BYTES
        ),
        name="average_down",
    )(coarse, fine_fields, owner.reshape(1, patches), target_tile.reshape(1, patches), tags)
    width = tile_count * EDGE + EDGE
    synced, signature = pl.pallas_call(
        functools.partial(finish, slabs),
        out_shape=(
            jax.ShapeDtypeStruct((FIELDS, tile_count, cells), f32),
            jax.ShapeDtypeStruct((1, width), f32),
        ),
        in_specs=[stay, vmem],
        out_specs=(stay, stay),
        scratch_shapes=[pltpu.VMEM((1, width), f32), pltpu.SemaphoreType.DMA((2,))],
        compiler_params=pltpu.CompilerParams(vmem_limit_bytes=VMEM_BYTES),
        name="write_outputs",
    )(synced, sums)
    return jnp.transpose(synced, (1, 0, 2)), signature


def solution(mesh):
    blocks, slabs = mesh.shape["blk"], mesh.shape["sig"]
    return jax.shard_map(
        functools.partial(shards, blocks, slabs),
        mesh=mesh,
        in_specs=(
            P(("blk", "sig"), None, None),
            P(("blk", "sig"), None, None, None),
            P(("blk", "sig"), None),
            P(("blk", "sig"), None),
            P(("blk", "sig"), None),
        ),
        out_specs=(P(("blk", "sig"), None, None), P("blk", None)),
        check_vma=False,
    )
```

time: 27.8 us -> 49.6 us (1.78)
  Pallas kernels: 20.6 us -> 48.8 us
  local copies, waits for them, and re-layouts: 6.27 us -> 0 us
    pallas_call x0 -> x1, Pallas kernels: none -> 25.6 us  [shards(): pl.pallas_call(functools.partial(finish, slabs), out_shape=(jax.ShapeDtyp...]
    unnamed x12 -> x0, local copies, waits for them, and re-layouts: 6.27 us -> none
    pallas_call x1, Pallas kernels: 20.6 us -> 23.1 us  [shards(): pl.pallas_call(functools.partial(kernel, blocks, slabs), out_shape=(jax.S...]
where the time goes in v2:
time: 49.6 us; the launch traced here: 49.4 us
  Pallas kernels  48.8 us (98%)
  between operations  0.64 us (1%)
    pallas_call x1, Pallas kernels, shards(): pl.pallas_call(functools.partial(finish, slabs), out_shape=(jax.ShapeDtyp...  25.6 us
    pallas_call x1, Pallas kernels, shards(): pl.pallas_call(functools.partial(kernel, blocks, slabs), out_shape=(jax.S...  23.1 us

profile of v2, /device:TPU:0, one launch (start us, length us, event | category | flops | bytes accessed | tf_op | source)
XLA Modules:
  0.0 49.4 jit_solution(520920534467736089)
XLA Ops:
  0.6 23.1 %average_down.1 = (f32[3,128,512]{2,1,0:T(8,128)}, f32[2,8,128]{2,1,0:T(8,128)}) custom-call(f32[3,128,512]{2,1,0:T(8,128)} %bitcast.4, f32[32,3,8,512]{3,2,1,0:T(8,128)} %fine_hbm.1, s32[1,32]{1,0:T(1,128)} %bitcast.5, s32[1,32]{1,0:T(1,128)} %bitcast.6, s32[128,512]{1,0:T(8,128)} %tags_hbm.1), custom_call_target="tpu_custom_call" | custom-call | tf_op jit(solution)/shard_map/average_down/pallas_call | solution.py:322
  23.8 25.6 %write_outputs.1 = (f32[3,128,512]{2,1,0:T(8,128)}, f32[1,1032]{1,0:T(1,128)}) custom-call(f32[3,128,512]{2,1,0:T(8,128)} %get-tuple-element.6.synced_in, f32[2,8,128]{2,1,0:T(8,128)} %get-tuple-element.7.sums), custom_call_target="tpu_custom_call" | custom-call | tf_op jit(solution)/shard_map/write_outputs/pallas_call | solution.py:358

commit v3 on v2

--- a/solution.py
+++ b/solution.py
@@ -9,16 +9,16 @@
 
 EDGE = 8
 FIELDS = 3
-VMEM_BYTES = 62 * 1024 * 1024
+VMEM_BYTES = 32 * 1024 * 1024
 MESH = pl.DeviceIdType.MESH
 
 
 def kernel(
     blocks, slabs,
     coarse_hbm, fine_hbm, owner_hbm, target_hbm, tags_hbm,
-    synced_hbm, sums_ref,
-    synced_ref, fine, coarse, tags, own_i, tgt_i, meta, rec, turned, tags_t, total, parts,
-    load_sem, out_sem, msend, mrecv, dsend, drecv, ssend, srecv,
+    synced_ref, sums_ref,
+    fine, coarse, tags, own_i, tgt_i, meta, rec, turned, tags_t, total, parts,
+    load_sem, msend, mrecv, dsend, drecv, ssend, srecv,
 ):
     tile_count = coarse.shape[1]
     cells = coarse.shape[2]
@@ -80,7 +80,6 @@
     pl.semaphore_wait(barrier, blocks - 1 + slabs - 1)
 
     started = []
-    writes = []
 
     def send(src, dst, send_sem, recv_sem, device):
         copy = pltpu.make_async_remote_copy(
@@ -108,10 +107,12 @@
             preferred_element_type=jnp.float32,
         )
 
-    def prepare():
+    def turn_tags():
         load_tags.wait()
         tags_t[...] = (0.25 * tags[...].astype(jnp.float32)).T.reshape(tags_t.shape)
         total[...] = jnp.zeros_like(total)
+
+    def prepare():
         for copy in metas:
             copy.wait_recv()
         if blocks <= 8:
@@ -133,8 +134,6 @@
     edge_row = jnp.zeros((1, EDGE, tile_count), jnp.float32)
 
     def weigh(f):
-        writes.append(pltpu.make_async_copy(synced_ref.at[f], synced_hbm.at[f], out_sem.at[f]))
-        writes[-1].start()
         turned[...] = synced_ref[f].T.reshape(turned.shape)
         for x in range(EDGE):
             mid = turned[x]
@@ -179,16 +178,14 @@
         def forward(f):
             came(f, "x0")
             go("d0", 2, 0, 1, 4, 6, f)
-            go("cx0", 2, 0, 1, 1, 3, f)
             came(f, "y1")
             go("d1", 4, 1, 1, 2, 6, f)
-            go("cy1", 4, 1, 1, 1, 5, f)
 
         def share(f):
             came(f, "x1")
-            go("cx1", 2, 1, 1, 1, 3, f)
+            go("cx", 2, 0, 2, 1, 3, f)
             came(f, "y0")
-            go("cy0", 4, 0, 1, 1, 5, f)
+            go("cy", 4, 0, 2, 1, 5, f)
 
         def share_diagonal(f):
             came(f, "d0")
@@ -196,12 +193,19 @@
             came(f, "d1")
             go("cd1", 6, 1, 1, 1, 7, f)
 
+        def drain(*later):
+            kept = [copies[name, FIELDS - 1] for name in later if (name, FIELDS - 1) in copies]
+            for copy in started:
+                if not any(copy is other for other in kept):
+                    copy.wait_send()
+            started[:] = kept
+
         def add_near(f):
             came(f, "c")
             add(0, f)
-            came(f, "cx0", "cx1")
+            came(f, "cx")
             add(1, f)
-            came(f, "cy0", "cy1")
+            came(f, "cy")
             add(2, f)
 
         def add_diagonal(f):
@@ -213,10 +217,11 @@
         average(1)
         own(1)
         average(2)
-        prepare()
         forward(0)
         own(2)
+        turn_tags()
         share(0)
+        prepare()
         forward(1)
         add_near(0)
         share(1)
@@ -228,6 +233,7 @@
         weigh(0)
         share_diagonal(1)
         add_near(2)
+        drain("d0", "d1", "cd0", "cd1")
         share_diagonal(2)
         add_diagonal(1)
         weigh(1)
@@ -243,6 +249,7 @@
                 rec.at[pl.ds(0, bit)], rec.at[pl.ds(bit, bit)], dsend.at[k], drecv.at[k], {"blk": partner(bit)}
             ).wait_recv()
             bit, k = 2 * bit, k + 1
+        turn_tags()
         prepare()
 
         def body(group, carry):
@@ -274,8 +281,6 @@
 
     for copy in started:
         copy.wait_send()
-    for copy in writes:
-        copy.wait()
 
 
 def finish(slabs, synced_in, sums, synced_out, signature, line, sem):
@@ -317,7 +322,7 @@
     coarse = jnp.transpose(coarse_fields, (1, 0, 2))
     stay = pl.BlockSpec(memory_space=pl.ANY)
     vmem = pl.BlockSpec(memory_space=pltpu.VMEM)
-    copies = 13 * FIELDS
+    copies = 11 * FIELDS
     f32 = jnp.float32
     synced, sums = pl.pallas_call(
         functools.partial(kernel, blocks, slabs),
@@ -326,9 +331,8 @@
             jax.ShapeDtypeStruct((2, EDGE, tile_count), f32),
         ),
         in_specs=[stay] * 5,
-        out_specs=(stay, vmem),
+        out_specs=(vmem, vmem),
         scratch_shapes=[
-            pltpu.VMEM((FIELDS, tile_count, cells), f32),
             pltpu.VMEM((FIELDS, patches, 8, cells), f32),
             pltpu.VMEM((FIELDS, tile_count, cells), f32),
             pltpu.VMEM((tile_count, cells), jnp.int32),
@@ -341,7 +345,6 @@
             pltpu.VMEM((EDGE, EDGE, tile_count), f32),
             pltpu.VMEM((slabs, 2, EDGE, tile_count), f32),
             pltpu.SemaphoreType.DMA((FIELDS + 4,)),
-            pltpu.SemaphoreType.DMA((FIELDS,)),
             pltpu.SemaphoreType.DMA((blocks,)),
             pltpu.SemaphoreType.DMA((blocks,)),
             pltpu.SemaphoreType.DMA((copies,)),
@@ -353,7 +356,10 @@
             collective_id=0, has_side_effects=True, vmem_limit_bytes=VMEM_BYTES
         ),
         name="average_down",
-    )(coarse, fine_fields, owner.reshape(1, patches), target_tile.reshape(1, patches), tags)
+    )(*[
+        pltpu.with_memory_space_constraint(x, pltpu.HBM)
+        for x in (coarse, fine_fields, owner.reshape(1, patches), target_tile.reshape(1, patches), tags)
+    ])
     width = tile_count * EDGE + EDGE
     synced, signature = pl.pallas_call(
         functools.partial(finish, slabs),
@@ -361,10 +367,9 @@
             jax.ShapeDtypeStruct((FIELDS, tile_count, cells), f32),
             jax.ShapeDtypeStruct((1, width), f32),
         ),
-        in_specs=[stay, vmem],
+        in_specs=[vmem, vmem],
         out_specs=(stay, stay),
         scratch_shapes=[pltpu.VMEM((1, width), f32), pltpu.SemaphoreType.DMA((2,))],
-        compiler_params=pltpu.CompilerParams(vmem_limit_bytes=VMEM_BYTES),
         name="write_outputs",
     )(synced, sums)
     return jnp.transpose(synced, (1, 0, 2)), signature

time: 49.6 us -> 25 us (0.50)
  Pallas kernels: 48.8 us -> 22.7 us
  local copies, waits for them, and re-layouts: 0 us -> 1.47 us
    pallas_call x1, Pallas kernels: 25.6 us -> 2.03 us  [shards(): pl.pallas_call(functools.partial(finish, slabs), out_shape=(jax.ShapeDtyp...]
    pallas_call x1, Pallas kernels: 23.1 us -> 20.7 us  [shards(): pl.pallas_call(functools.partial(kernel, blocks, slabs), out_shape=(jax.S...]
    unnamed x0 -> x4, local copies, waits for them, and re-layouts: none -> 1.47 us
where the time goes in v3:
time: 25 us; the launch traced here: 24.9 us
  Pallas kernels  22.7 us (91%)
  local copies, waits for them, and re-layouts  1.47 us (6%)
  between operations  0.65 us (3%)
    pallas_call x1, Pallas kernels, shards(): pl.pallas_call(functools.partial(kernel, blocks, slabs), out_shape=(jax.S...  20.7 us
    pallas_call x1, Pallas kernels, shards(): pl.pallas_call(functools.partial(finish, slabs), out_shape=(jax.ShapeDtyp...  2.03 us
    unnamed x4, local copies, waits for them, and re-layouts  1.47 us

profile of v3, /device:TPU:0, one launch (start us, length us, event | category | flops | bytes accessed | tf_op | source)
XLA Modules:
  0.0 24.9 jit_solution(4444011228156956628)
XLA Ops:
  0.6 20.7 %average_down.1 = (f32[3,128,512]{2,1,0:T(8,128)S(1)}, f32[2,8,128]{2,1,0:T(8,128)S(1)}) custom-call(f32[3,128,512]{2,1,0:T(8,128)} %bitcast.4, f32[32,3,8,512]{3,2,1,0:T(8,128)} %fine_hbm.1, s32[1,32]{1,0:T(1,128)} %bitcast.5, s32[1,32]{1,0:T(1,128)} %bitcast.6, s32[128,512]{1,0:T(8,128)} %tags_hbm.1), custom_call_target="tpu_custom_call" | custom-call | tf_op jit(solution)/shard_map/average_down/pallas_call | solution.py:327
  21.3 0.0 copy-start
  21.4 0.9 %copy-done = f32[3,128,512]{2,1,0:T(8,128)} copy-done((f32[3,128,512]{2,1,0:T(8,128)}, f32[3,128,512]{2,1,0:T(8,128)S(1)}, u32[]{:S(2)}) %copy-start) | copy-done | bytes 786456
  22.2 0.0 copy-start.1
  22.2 0.6 %copy-done.1 = f32[2,8,128]{2,1,0:T(8,128)} copy-done((f32[2,8,128]{2,1,0:T(8,128)}, f32[2,8,128]{2,1,0:T(8,128)S(1)}, u32[]{:S(2)}) %copy-start.1) | copy-done | bytes 8216
  22.8 2.0 %write_outputs.1 = (f32[3,128,512]{2,1,0:T(8,128)}, f32[1,1032]{1,0:T(1,128)}) custom-call(f32[3,128,512]{2,1,0:T(8,128)} %copy-done, f32[2,8,128]{2,1,0:T(8,128)} %copy-done.1), custom_call_target="tpu_custom_call" | custom-call | tf_op jit(solution)/shard_map/write_outputs/pallas_call | solution.py:364
Async XLA Ops:
  21.3 0.9 %copy-start = (f32[3,128,512]{2,1,0:T(8,128)}, f32[3,128,512]{2,1,0:T(8,128)S(1)}, u32[]{:S(2)}) copy-start(f32[3,128,512]{2,1,0:T(8,128)S(1)} %get-tuple-element.6.synced_in) | copy-start | bytes 2359300
  22.2 0.6 %copy-start.1 = (f32[2,8,128]{2,1,0:T(8,128)}, f32[2,8,128]{2,1,0:T(8,128)S(1)}, u32[]{:S(2)}) copy-start(f32[2,8,128]{2,1,0:T(8,128)S(1)} %get-tuple-element.7.sums) | copy-start | bytes 24580

commit v4 on v3

--- a/solution.py
+++ b/solution.py
@@ -9,6 +9,7 @@
 
 EDGE = 8
 FIELDS = 3
+PIECES = 4
 VMEM_BYTES = 32 * 1024 * 1024
 MESH = pl.DeviceIdType.MESH
 
@@ -40,11 +41,19 @@
         copy.start()
         return copy
 
-    load_fine = [load(f, fine_hbm.at[:, f], fine.at[f]) for f in range(FIELDS)]
-    load_owner = load(FIELDS, owner_hbm, own_i)
-    load_target = load(FIELDS + 1, target_hbm, tgt_i)
-    load_tags = load(FIELDS + 2, tags_hbm, tags)
-    load_coarse = load(FIELDS + 3, coarse_hbm, coarse)
+    piece = patches // PIECES
+    load_fine = [
+        [
+            load(f * PIECES + k, fine_hbm.at[pl.ds(k * piece, piece), f], fine.at[f, pl.ds(k * piece, piece)])
+            for k in range(PIECES)
+        ]
+        for f in range(FIELDS)
+    ]
+    k = FIELDS * PIECES
+    load_owner = load(k, owner_hbm, own_i)
+    load_target = load(k + 1, target_hbm, tgt_i)
+    load_tags = load(k + 2, tags_hbm, tags)
+    load_coarse = [load(k + 3 + f, coarse_hbm.at[f], coarse.at[f]) for f in range(FIELDS)]
 
     barrier = pltpu.get_barrier_semaphore()
     for mask in range(1, blocks):
@@ -65,7 +74,8 @@
     ).astype(jnp.bfloat16)
 
     def average(f):
-        load_fine[f].wait()
+        for copy in load_fine[f]:
+            copy.wait()
         high, low = split(fine[f].reshape(patches * 8, cells))
         rows = jnp.dot(mean, high, preferred_element_type=jnp.float32)
         rows = rows + jnp.dot(mean, low, preferred_element_type=jnp.float32)
@@ -125,8 +135,8 @@
                 jnp.zeros((tile_count, 4 * patches), jnp.float32),
             )
         free = jnp.max(hits, axis=1, keepdims=True) == 0
-        load_coarse.wait()
         for f in range(FIELDS):
+            load_coarse[f].wait()
             synced_ref[f] = jnp.where(free, coarse[f], 0.0)
 
     depth = lax.broadcasted_iota(jnp.int32, (EDGE, EDGE, tile_count), 1)
@@ -284,36 +294,41 @@
 
 
 def finish(slabs, synced_in, sums, synced_out, signature, line, sem):
-    write = pltpu.make_async_copy(synced_in, synced_out, sem.at[0])
-    write.start()
     tile_count = sums.shape[2]
+    writes = []
+    piece = tile_count // PIECES
+    for f in range(FIELDS):
+        for k in range(PIECES):
+            rows = pl.ds(k * piece, piece)
+            writes.append(
+                pltpu.make_async_copy(
+                    synced_in.at[f, rows], synced_out.at[f, rows], sem.at[1 + f * PIECES + k]
+                )
+            )
+            writes[-1].start()
     along_y = sums[0] * (1.0 / (EDGE * EDGE * slabs))
     along_z = sums[1] * (1.0 / (EDGE * EDGE * tile_count * slabs))
     group = 128 // EDGE
+    lines = tile_count // group
     spread = jnp.concatenate([along_y] * group, axis=0)
     row = lax.broadcasted_iota(jnp.int32, (128, tile_count), 0)
     col = lax.broadcasted_iota(jnp.int32, (128, tile_count), 1)
     spread = jnp.where(col % group == row // EDGE, spread, 0.0)
-    lines = tile_count // group
-    pick = (
-        lax.broadcasted_iota(jnp.int32, (lines, tile_count), 1) // group
-        == lax.broadcasted_iota(jnp.int32, (lines, tile_count), 0)
-    ).astype(jnp.float32)
-    across = (((1,), (1,)), ((), ()))
-    order = lax.dot_general(
-        pick, spread, across, precision=lax.Precision.HIGHEST, preferred_element_type=jnp.float32
-    )
-    last = lax.dot_general(
-        jnp.ones((8, tile_count), jnp.float32), along_z, across,
-        precision=lax.Precision.HIGHEST, preferred_element_type=jnp.float32,
-    )
+    terms = jnp.concatenate([spread, along_z], axis=0)
+    high = terms.astype(jnp.bfloat16).astype(jnp.float32)
+    terms = jnp.concatenate([high, terms - high], axis=1).astype(jnp.bfloat16)
+    row = lax.broadcasted_iota(jnp.int32, (2 * lines, 2 * tile_count), 0)
+    col = lax.broadcasted_iota(jnp.int32, (2 * lines, 2 * tile_count), 1) % tile_count
+    pick = jnp.where((col // group == row) | (row >= lines), 1.0, 0.0).astype(jnp.bfloat16)
+    order = lax.dot_general(pick, terms, (((1,), (1,)), ((), ())), preferred_element_type=jnp.float32)
     for r in range(lines):
-        line[0:1, r * 128 : (r + 1) * 128] = order[r : r + 1]
-    line[0:1, lines * 128 : lines * 128 + EDGE] = last[0:1]
-    write_line = pltpu.make_async_copy(line, signature, sem.at[1])
+        line[0:1, r * 128 : (r + 1) * 128] = order[r : r + 1, :128]
+    line[0:1, lines * 128 : lines * 128 + EDGE] = order[lines : lines + 1, 128:]
+    write_line = pltpu.make_async_copy(line, signature, sem.at[0])
     write_line.start()
+    for copy in writes:
+        copy.wait()
     write_line.wait()
-    write.wait()
 
 
 def shards(blocks, slabs, coarse_fields, fine_fields, owner, target_tile, tags):
@@ -344,7 +359,7 @@
             pltpu.VMEM((EDGE, EDGE, EDGE, tile_count), f32),
             pltpu.VMEM((EDGE, EDGE, tile_count), f32),
             pltpu.VMEM((slabs, 2, EDGE, tile_count), f32),
-            pltpu.SemaphoreType.DMA((FIELDS + 4,)),
+            pltpu.SemaphoreType.DMA((FIELDS * PIECES + 3 + FIELDS,)),
             pltpu.SemaphoreType.DMA((blocks,)),
             pltpu.SemaphoreType.DMA((blocks,)),
             pltpu.SemaphoreType.DMA((copies,)),
@@ -369,7 +384,8 @@
         ),
         in_specs=[vmem, vmem],
         out_specs=(stay, stay),
-        scratch_shapes=[pltpu.VMEM((1, width), f32), pltpu.SemaphoreType.DMA((2,))],
+        scratch_shapes=[pltpu.VMEM((1, width), f32), pltpu.SemaphoreType.DMA((1 + FIELDS * PIECES,))],
+        compiler_params=pltpu.CompilerParams(vmem_limit_bytes=4 * 1024 * 1024),
         name="write_outputs",
     )(synced, sums)
     return jnp.transpose(synced, (1, 0, 2)), signature

time: 25 us -> 22.6 us (0.904)
  local copies, waits for them, and re-layouts: 1.47 us -> 0 us
  Pallas kernels: 22.7 us -> 21.8 us
    unnamed x4 -> x0, local copies, waits for them, and re-layouts: 1.47 us -> none
    pallas_call x1, Pallas kernels: 2.03 us -> 0.98 us  [shards(): pl.pallas_call(functools.partial(finish, slabs), out_shape=(jax.ShapeDtyp...]
where the time goes in v4:
time: 22.6 us; the launch traced here: 22.4 us
  Pallas kernels  21.8 us (96%)
  between operations  0.64 us (3%)
    pallas_call x1, Pallas kernels, shards(): pl.pallas_call(functools.partial(kernel, blocks, slabs), out_shape=(jax.S...  20.8 us
    pallas_call x1, Pallas kernels, shards(): pl.pallas_call(functools.partial(finish, slabs), out_shape=(jax.ShapeDtyp...  0.98 us

profile of v4, /device:TPU:0, one launch (start us, length us, event | category | flops | bytes accessed | tf_op | source)
XLA Modules:
  0.0 22.4 jit_solution(2495218383843455030)
XLA Ops:
  0.6 20.8 %average_down.1 = (f32[3,128,512]{2,1,0:T(8,128)S(1)}, f32[2,8,128]{2,1,0:T(8,128)S(1)}) custom-call(f32[3,128,512]{2,1,0:T(8,128)} %bitcast.4, f32[32,3,8,512]{3,2,1,0:T(8,128)} %fine_hbm.1, s32[1,32]{1,0:T(1,128)} %bitcast.5, s32[1,32]{1,0:T(1,128)} %bitcast.6, s32[128,512]{1,0:T(8,128)} %tags_hbm.1), custom_call_target="tpu_custom_call" | custom-call | tf_op jit(solution)/shard_map/average_down/pallas_call | solution.py:342
  21.5 1.0 %write_outputs.1 = (f32[3,128,512]{2,1,0:T(8,128)}, f32[1,1032]{1,0:T(1,128)}) custom-call(f32[3,128,512]{2,1,0:T(8,128)S(1)} %get-tuple-element.6.synced_in, f32[2,8,128]{2,1,0:T(8,128)S(1)} %get-tuple-element.7.sums), custom_call_target="tpu_custom_call" | custom-call | tf_op jit(solution)/shard_map/write_outputs/pallas_call | solution.py:379

commit v5 on v4

--- a/solution.py
+++ b/solution.py
@@ -18,7 +18,7 @@
     blocks, slabs,
     coarse_hbm, fine_hbm, owner_hbm, target_hbm, tags_hbm,
     synced_ref, sums_ref,
-    fine, coarse, tags, own_i, tgt_i, meta, rec, turned, tags_t, total, parts,
+    fine, coarse, tags, own_i, tgt_i, meta, rec, chosen, turned, tags_t, total, parts,
     load_sem, msend, mrecv, dsend, drecv, ssend, srecv,
 ):
     tile_count = coarse.shape[1]
@@ -81,7 +81,8 @@
         rows = rows + jnp.dot(mean, low, preferred_element_type=jnp.float32)
         rec[0, f] = rows.reshape(rec.shape[2:])
 
-    average(0)
+    for f in range(FIELDS - 1):
+        average(f)
     load_owner.wait()
     load_target.wait()
     code = own_i[...] * tile_count + tgt_i[...]
@@ -100,21 +101,21 @@
         started.append(copy)
         return copy
 
-    lane = lax.broadcasted_iota(jnp.int32, (tile_count, 4 * patches), 1)
-    first = (lane // patches) % 2 == 0
+    lane = lax.broadcasted_iota(jnp.int32, (1, 4 * patches), 1) // patches
     tile_codes = (
         lax.broadcasted_iota(jnp.int32, (tile_count, 4 * patches), 0) + me * tile_count
     ).astype(jnp.float32)
 
-    def place(group):
-        codes = jnp.where(first, meta[2 * group][0:1], meta[2 * group + 1][0:1])
+    def place(slots):
+        codes = meta[slots[0]][0:1]
+        for k in range(1, 4):
+            codes = jnp.where(lane == k, meta[slots[k]][0:1], codes)
         return jnp.where(codes == tile_codes, 1.0, 0.0).astype(jnp.float32)
 
-    def add(group, f):
-        rows = rec[pl.ds(2 * group, 2), f].reshape(2 * patches, cells)
+    def add(chosen, slot, count, f):
+        rows = rec[pl.ds(slot, count), f].reshape(count * patches, cells)
         synced_ref[f] += jnp.dot(
-            place(group).astype(jnp.bfloat16), jnp.concatenate(split(rows), axis=0),
-            preferred_element_type=jnp.float32,
+            chosen, jnp.concatenate(split(rows), axis=0), preferred_element_type=jnp.float32
         )
 
     def turn_tags():
@@ -125,13 +126,15 @@
     def prepare():
         for copy in metas:
             copy.wait_recv()
-        if blocks <= 8:
-            hits = place(0)
-            for group in range(1, blocks // 2):
-                hits = hits + place(group)
+        if blocks == 8:
+            hits = None
+            for k, slots in enumerate(((0, 1, 2, 3), (4, 5, 0, 1), (2, 3, 4, 5), (6, 7, 6, 7))):
+                found = place(slots)
+                chosen[:, k * 128 : (k + 1) * 128] = found.astype(jnp.bfloat16)
+                hits = found if hits is None else jnp.maximum(hits, found)
         else:
             hits = lax.fori_loop(
-                0, blocks // 2, lambda group, found: found + place(group),
+                0, blocks // 4, lambda k, found: found + place([4 * k, 4 * k + 1, 4 * k + 2, 4 * k + 3]),
                 jnp.zeros((tile_count, 4 * patches), jnp.float32),
             )
         free = jnp.max(hits, axis=1, keepdims=True) == 0
@@ -167,92 +170,85 @@
     if blocks == 8:
         copies = {}
 
-        def go(name, slot, start, count, mask, target, f):
+        def go(name, slot, start, count, mask, target, part):
             k = len(copies)
-            copies[name, f] = send(
-                rec.at[slot, f, pl.ds(start, count)], rec.at[target, f, pl.ds(start, count)],
+            low, high = part
+            fields, halves = pl.ds(low, high - low), pl.ds(start, count)
+            copies[name, part] = send(
+                rec.at[slot, fields, halves], rec.at[target, fields, halves],
                 dsend.at[k], drecv.at[k], {"blk": partner(mask)},
             )
 
-        def came(f, *names):
+        def came(part, *names):
             for name in names:
-                copies[name, f].wait_recv()
-
-        def own(f):
-            go("x0", 0, 0, 1, 2, 2, f)
-            go("y1", 0, 1, 1, 4, 4, f)
-            go("x1", 0, 1, 1, 2, 2, f)
-            go("y0", 0, 0, 1, 4, 4, f)
-            go("c", 0, 0, 2, 1, 1, f)
-
-        def forward(f):
-            came(f, "x0")
-            go("d0", 2, 0, 1, 4, 6, f)
-            came(f, "y1")
-            go("d1", 4, 1, 1, 2, 6, f)
-
-        def share(f):
-            came(f, "x1")
-            go("cx", 2, 0, 2, 1, 3, f)
-            came(f, "y0")
-            go("cy", 4, 0, 2, 1, 5, f)
-
-        def share_diagonal(f):
-            came(f, "d0")
-            go("cd0", 6, 0, 1, 1, 7, f)
-            came(f, "d1")
-            go("cd1", 6, 1, 1, 1, 7, f)
-
-        def drain(*later):
-            kept = [copies[name, FIELDS - 1] for name in later if (name, FIELDS - 1) in copies]
+                copies[name, part].wait_recv()
+
+        def own(part):
+            go("x0", 0, 0, 1, 2, 2, part)
+            go("y1", 0, 1, 1, 4, 4, part)
+            go("x1", 0, 1, 1, 2, 2, part)
+            go("y0", 0, 0, 1, 4, 4, part)
+            go("c", 0, 0, 2, 1, 1, part)
+
+        def forward(part):
+            came(part, "x0")
+            go("d0", 2, 0, 1, 4, 6, part)
+            came(part, "y1")
+            go("d1", 4, 1, 1, 2, 6, part)
+
+        def share(part):
+            came(part, "x1")
+            go("cx", 2, 0, 2, 1, 3, part)
+            came(part, "y0")
+            go("cy", 4, 0, 2, 1, 5, part)
+
+        def share_diagonal(part):
+            came(part, "d0")
+            go("cd0", 6, 0, 1, 1, 7, part)
+            came(part, "d1")
+            go("cd1", 6, 1, 1, 1, 7, part)
+
+        def drain(part, *later):
+            kept = [copies[name, part] for name in later if (name, part) in copies]
             for copy in started:
                 if not any(copy is other for other in kept):
                     copy.wait_send()
             started[:] = kept
 
-        def add_near(f):
-            came(f, "c")
-            add(0, f)
-            came(f, "cx")
-            add(1, f)
-            came(f, "cy")
-            add(2, f)
-
-        def add_diagonal(f):
-            came(f, "cd0", "cd1")
-            add(3, f)
-
-        own(0)
+        def add_near(part):
+            came(part, "c", "cx", "cy")
+            for f in range(*part):
+                add(chosen[:, :384], 0, 6, f)
+
+        def add_diagonal(part):
+            came(part, "cd0", "cd1")
+            for f in range(*part):
+                add(chosen[:, 384:], 6, 2, f)
+
+        early, late = (0, FIELDS - 1), (FIELDS - 1, FIELDS)
+        own(early)
         send_metas()
-        average(1)
-        own(1)
-        average(2)
-        forward(0)
-        own(2)
+        average(FIELDS - 1)
+        own(late)
         turn_tags()
-        share(0)
+        forward(early)
+        share(early)
+        forward(late)
         prepare()
-        forward(1)
-        add_near(0)
-        share(1)
-        share_diagonal(0)
-        forward(2)
-        add_near(1)
-        share(2)
-        add_diagonal(0)
-        weigh(0)
-        share_diagonal(1)
-        add_near(2)
-        drain("d0", "d1", "cd0", "cd1")
-        share_diagonal(2)
-        add_diagonal(1)
-        weigh(1)
-        add_diagonal(2)
-        weigh(2)
+        share(late)
+        add_near(early)
+        share_diagonal(early)
+        add_near(late)
+        add_diagonal(early)
+        drain(late, "d0", "d1")
+        share_diagonal(late)
+        for f in range(*early):
+            weigh(f)
+        add_diagonal(late)
+        weigh(FIELDS - 1)
     else:
         send_metas()
-        average(1)
-        average(2)
+        average(FIELDS - 1)
         bit, k = 1, 0
         while bit < blocks:
             send(
@@ -263,8 +259,9 @@
         prepare()
 
         def body(group, carry):
+            pair = place([2 * group, 2 * group + 1, 2 * group, 2 * group + 1]).astype(jnp.bfloat16)
             for f in range(FIELDS):
-                add(group, f)
+                add(pair, 2 * group, 2, f)
             return carry
 
         lax.fori_loop(0, blocks // 2, body, 0)
@@ -337,7 +334,7 @@
     coarse = jnp.transpose(coarse_fields, (1, 0, 2))
     stay = pl.BlockSpec(memory_space=pl.ANY)
     vmem = pl.BlockSpec(memory_space=pltpu.VMEM)
-    copies = 11 * FIELDS
+    copies = 22
     f32 = jnp.float32
     synced, sums = pl.pallas_call(
         functools.partial(kernel, blocks, slabs),
@@ -355,6 +352,7 @@
             pltpu.VMEM((1, patches), jnp.int32),
             pltpu.VMEM((blocks, 8, 128), f32),
             pltpu.VMEM((blocks, FIELDS, 2, patches // 2, cells), f32),
+            pltpu.VMEM((tile_count, 512), jnp.bfloat16),
             pltpu.VMEM((EDGE, EDGE, EDGE, tile_count), f32),
             pltpu.VMEM((EDGE, EDGE, EDGE, tile_count), f32),
             pltpu.VMEM((EDGE, EDGE, tile_count), f32),

time: 22.6 us -> 22.3 us (0.987)
  Pallas kernels: 21.8 us -> 21.5 us
    pallas_call x1, Pallas kernels: 20.8 us -> 20.5 us  [shards(): pl.pallas_call(functools.partial(kernel, blocks, slabs), out_shape=(jax.S...]
where the time goes in v5:
time: 22.3 us; the launch traced here: 22.2 us
  Pallas kernels  21.5 us (96%)
  between operations  0.64 us (3%)
    pallas_call x1, Pallas kernels, shards(): pl.pallas_call(functools.partial(kernel, blocks, slabs), out_shape=(jax.S...  20.5 us
    pallas_call x1, Pallas kernels, shards(): pl.pallas_call(functools.partial(finish, slabs), out_shape=(jax.ShapeDtyp...  0.98 us

profile of v5, /device:TPU:0, one launch (start us, length us, event | category | flops | bytes accessed | tf_op | source)
XLA Modules:
  0.0 22.2 jit_solution(5121707487238712225)
XLA Ops:
  0.6 20.5 %average_down.1 = (f32[3,128,512]{2,1,0:T(8,128)S(1)}, f32[2,8,128]{2,1,0:T(8,128)S(1)}) custom-call(f32[3,128,512]{2,1,0:T(8,128)} %bitcast.4, f32[32,3,8,512]{3,2,1,0:T(8,128)} %fine_hbm.1, s32[1,32]{1,0:T(1,128)} %bitcast.5, s32[1,32]{1,0:T(1,128)} %bitcast.6, s32[128,512]{1,0:T(8,128)} %tags_hbm.1), custom_call_target="tpu_custom_call" | custom-call | tf_op jit(solution)/shard_map/average_down/pallas_call | solution.py:339
  21.2 1.0 %write_outputs.1 = (f32[3,128,512]{2,1,0:T(8,128)}, f32[1,1032]{1,0:T(1,128)}) custom-call(f32[3,128,512]{2,1,0:T(8,128)S(1)} %get-tuple-element.6.synced_in, f32[2,8,128]{2,1,0:T(8,128)S(1)} %get-tuple-element.7.sums), custom_call_target="tpu_custom_call" | custom-call | tf_op jit(solution)/shard_map/write_outputs/pallas_call | solution.py:377

commit v6 on v5

--- a/solution.py
+++ b/solution.py
@@ -81,8 +81,7 @@
         rows = rows + jnp.dot(mean, low, preferred_element_type=jnp.float32)
         rec[0, f] = rows.reshape(rec.shape[2:])
 
-    for f in range(FIELDS - 1):
-        average(f)
+    average(0)
     load_owner.wait()
     load_target.wait()
     code = own_i[...] * tile_count + tgt_i[...]
@@ -188,18 +187,21 @@
             go("y1", 0, 1, 1, 4, 4, part)
             go("x1", 0, 1, 1, 2, 2, part)
             go("y0", 0, 0, 1, 4, 4, part)
-            go("c", 0, 0, 2, 1, 1, part)
-
-        def forward(part):
-            came(part, "x0")
+
+        def forward(part, *pieces):
+            for piece in pieces:
+                came(piece, "x0")
             go("d0", 2, 0, 1, 4, 6, part)
-            came(part, "y1")
+            for piece in pieces:
+                came(piece, "y1")
             go("d1", 4, 1, 1, 2, 6, part)
 
-        def share(part):
-            came(part, "x1")
+        def share(part, *pieces):
+            for piece in pieces:
+                came(piece, "x1")
             go("cx", 2, 0, 2, 1, 3, part)
-            came(part, "y0")
+            for piece in pieces:
+                came(piece, "y0")
             go("cy", 4, 0, 2, 1, 5, part)
 
         def share_diagonal(part):
@@ -226,29 +228,36 @@
                 add(chosen[:, 384:], 6, 2, f)
 
         early, late = (0, FIELDS - 1), (FIELDS - 1, FIELDS)
-        own(early)
+        pieces = [(f, f + 1) for f in range(FIELDS - 1)]
+        own(pieces[0])
         send_metas()
+        for piece in pieces[1:]:
+            average(piece[0])
+            own(piece)
+        go("c", 0, 0, 2, 1, 1, early)
         average(FIELDS - 1)
+        forward(early, *pieces)
         own(late)
+        go("c", 0, 0, 2, 1, 1, late)
         turn_tags()
-        forward(early)
-        share(early)
-        forward(late)
+        share(early, *pieces)
         prepare()
-        share(late)
         add_near(early)
+        forward(late, late)
         share_diagonal(early)
+        share(late, late)
+        add_diagonal(early)
+        for f in range(*early):
+            weigh(f)
         add_near(late)
-        add_diagonal(early)
         drain(late, "d0", "d1")
         share_diagonal(late)
-        for f in range(*early):
-            weigh(f)
         add_diagonal(late)
         weigh(FIELDS - 1)
     else:
         send_metas()
-        average(FIELDS - 1)
+        for f in range(1, FIELDS):
+            average(f)
         bit, k = 1, 0
         while bit < blocks:
             send(
@@ -334,7 +343,7 @@
     coarse = jnp.transpose(coarse_fields, (1, 0, 2))
     stay = pl.BlockSpec(memory_space=pl.ANY)
     vmem = pl.BlockSpec(memory_space=pltpu.VMEM)
-    copies = 22
+    copies = 26
     f32 = jnp.float32
     synced, sums = pl.pallas_call(
         functools.partial(kernel, blocks, slabs),

time: 22.3 us -> 23.3 us (1.045)
  Pallas kernels: 21.5 us -> 22.5 us
    pallas_call x1, Pallas kernels: 20.5 us -> 21.5 us  [shards(): pl.pallas_call(functools.partial(kernel, blocks, slabs), out_shape=(jax.S...]
where the time goes in v6:
time: 23.3 us; the launch traced here: 23.2 us
  Pallas kernels  22.5 us (97%)
  between operations  0.64 us (3%)
    pallas_call x1, Pallas kernels, shards(): pl.pallas_call(functools.partial(kernel, blocks, slabs), out_shape=(jax.S...  21.5 us
    pallas_call x1, Pallas kernels, shards(): pl.pallas_call(functools.partial(finish, slabs), out_shape=(jax.ShapeDtyp...  0.98 us

profile of v6, /device:TPU:0, one launch (start us, length us, event | category | flops | bytes accessed | tf_op | source)
XLA Modules:
  0.0 23.2 jit_solution(518916001776917305)
XLA Ops:
  0.6 21.5 %average_down.1 = (f32[3,128,512]{2,1,0:T(8,128)S(1)}, f32[2,8,128]{2,1,0:T(8,128)S(1)}) custom-call(f32[3,128,512]{2,1,0:T(8,128)} %bitcast.4, f32[32,3,8,512]{3,2,1,0:T(8,128)} %fine_hbm.1, s32[1,32]{1,0:T(1,128)} %bitcast.5, s32[1,32]{1,0:T(1,128)} %bitcast.6, s32[128,512]{1,0:T(8,128)} %tags_hbm.1), custom_call_target="tpu_custom_call" | custom-call | tf_op jit(solution)/shard_map/average_down/pallas_call | solution.py:348
  22.2 1.0 %write_outputs.1 = (f32[3,128,512]{2,1,0:T(8,128)}, f32[1,1032]{1,0:T(1,128)}) custom-call(f32[3,128,512]{2,1,0:T(8,128)S(1)} %get-tuple-element.6.synced_in, f32[2,8,128]{2,1,0:T(8,128)S(1)} %get-tuple-element.7.sums), custom_call_target="tpu_custom_call" | custom-call | tf_op jit(solution)/shard_map/write_outputs/pallas_call | solution.py:386

commit v7 on v6

--- a/solution.py
+++ b/solution.py
@@ -230,28 +230,28 @@
         early, late = (0, FIELDS - 1), (FIELDS - 1, FIELDS)
         pieces = [(f, f + 1) for f in range(FIELDS - 1)]
         own(pieces[0])
-        send_metas()
         for piece in pieces[1:]:
             average(piece[0])
             own(piece)
+        send_metas()
+        average(FIELDS - 1)
+        own(late)
         go("c", 0, 0, 2, 1, 1, early)
-        average(FIELDS - 1)
-        forward(early, *pieces)
-        own(late)
         go("c", 0, 0, 2, 1, 1, late)
         turn_tags()
+        forward(early, *pieces)
         share(early, *pieces)
+        forward(late, late)
         prepare()
+        share(late, late)
         add_near(early)
-        forward(late, late)
         share_diagonal(early)
-        share(late, late)
+        add_near(late)
         add_diagonal(early)
+        drain(late, "d0", "d1")
+        share_diagonal(late)
         for f in range(*early):
             weigh(f)
-        add_near(late)
-        drain(late, "d0", "d1")
-        share_diagonal(late)
         add_diagonal(late)
         weigh(FIELDS - 1)
     else:

time: 23.3 us -> 22.7 us (0.974)
  Pallas kernels: 22.5 us -> 21.9 us
    pallas_call x1, Pallas kernels: 21.5 us -> 20.9 us  [shards(): pl.pallas_call(functools.partial(kernel, blocks, slabs), out_shape=(jax.S...]
where the time goes in v7:
time: 22.7 us; the launch traced here: 22.5 us
  Pallas kernels  21.9 us (96%)
  between operations  0.64 us (3%)
    pallas_call x1, Pallas kernels, shards(): pl.pallas_call(functools.partial(kernel, blocks, slabs), out_shape=(jax.S...  20.9 us
    pallas_call x1, Pallas kernels, shards(): pl.pallas_call(functools.partial(finish, slabs), out_shape=(jax.ShapeDtyp...  0.98 us

profile of v7, /device:TPU:0, one launch (start us, length us, event | category | flops | bytes accessed | tf_op | source)
XLA Modules:
  0.0 22.5 jit_solution(2875891452901678275)
XLA Ops:
  0.6 20.9 %average_down.1 = (f32[3,128,512]{2,1,0:T(8,128)S(1)}, f32[2,8,128]{2,1,0:T(8,128)S(1)}) custom-call(f32[3,128,512]{2,1,0:T(8,128)} %bitcast.4, f32[32,3,8,512]{3,2,1,0:T(8,128)} %fine_hbm.1, s32[1,32]{1,0:T(1,128)} %bitcast.5, s32[1,32]{1,0:T(1,128)} %bitcast.6, s32[128,512]{1,0:T(8,128)} %tags_hbm.1), custom_call_target="tpu_custom_call" | custom-call | tf_op jit(solution)/shard_map/average_down/pallas_call | solution.py:348
  21.5 1.0 %write_outputs.1 = (f32[3,128,512]{2,1,0:T(8,128)}, f32[1,1032]{1,0:T(1,128)}) custom-call(f32[3,128,512]{2,1,0:T(8,128)S(1)} %get-tuple-element.6.synced_in, f32[2,8,128]{2,1,0:T(8,128)S(1)} %get-tuple-element.7.sums), custom_call_target="tpu_custom_call" | custom-call | tf_op jit(solution)/shard_map/write_outputs/pallas_call | solution.py:386

commit v8 on v5

--- a/solution.py
+++ b/solution.py
@@ -41,19 +41,7 @@
         copy.start()
         return copy
 
-    piece = patches // PIECES
-    load_fine = [
-        [
-            load(f * PIECES + k, fine_hbm.at[pl.ds(k * piece, piece), f], fine.at[f, pl.ds(k * piece, piece)])
-            for k in range(PIECES)
-        ]
-        for f in range(FIELDS)
-    ]
-    k = FIELDS * PIECES
-    load_owner = load(k, owner_hbm, own_i)
-    load_target = load(k + 1, target_hbm, tgt_i)
-    load_tags = load(k + 2, tags_hbm, tags)
-    load_coarse = [load(k + 3 + f, coarse_hbm.at[f], coarse.at[f]) for f in range(FIELDS)]
+    load_fine = [load(f, fine_hbm.at[:, f], fine.at[f]) for f in range(FIELDS - 1)]
 
     barrier = pltpu.get_barrier_semaphore()
     for mask in range(1, blocks):
@@ -63,6 +51,12 @@
             barrier, inc=1, device_id={"sig": lax.rem(slab + shift, slabs)}, device_id_type=MESH
         )
 
+    load_owner = load(FIELDS, owner_hbm, own_i)
+    load_target = load(FIELDS + 1, target_hbm, tgt_i)
+    load_fine.append(load(FIELDS - 1, fine_hbm.at[:, FIELDS - 1], fine.at[FIELDS - 1]))
+    load_tags = load(FIELDS + 2, tags_hbm, tags)
+    load_coarse = load(FIELDS + 3, coarse_hbm, coarse)
+
     def split(x):
         high = x.astype(jnp.bfloat16)
         return high, (x - high.astype(jnp.float32)).astype(jnp.bfloat16)
@@ -74,8 +68,7 @@
     ).astype(jnp.bfloat16)
 
     def average(f):
-        for copy in load_fine[f]:
-            copy.wait()
+        load_fine[f].wait()
         high, low = split(fine[f].reshape(patches * 8, cells))
         rows = jnp.dot(mean, high, preferred_element_type=jnp.float32)
         rows = rows + jnp.dot(mean, low, preferred_element_type=jnp.float32)
@@ -138,8 +131,8 @@
                 jnp.zeros((tile_count, 4 * patches), jnp.float32),
             )
         free = jnp.max(hits, axis=1, keepdims=True) == 0
+        load_coarse.wait()
         for f in range(FIELDS):
-            load_coarse[f].wait()
             synced_ref[f] = jnp.where(free, coarse[f], 0.0)
 
     depth = lax.broadcasted_iota(jnp.int32, (EDGE, EDGE, tile_count), 1)
@@ -169,6 +162,7 @@
 
     if blocks == 8:
         copies = {}
+        early, late = (0, FIELDS - 1), (FIELDS - 1, FIELDS)
 
         def go(name, slot, start, count, mask, target, part):
             k = len(copies)
@@ -204,9 +198,13 @@
 
         def share_diagonal(part):
             came(part, "d0")
-            go("cd0", 6, 0, 1, 1, 7, part)
+            if part == late:
+                go("cd0", 6, 0, 1, 1, 7, part)
             came(part, "d1")
-            go("cd1", 6, 1, 1, 1, 7, part)
+            if part == late:
+                go("cd1", 6, 1, 1, 1, 7, part)
+            else:
+                go("cd", 6, 0, 2, 1, 7, part)
 
         def drain(part, *later):
             kept = [copies[name, part] for name in later if (name, part) in copies]
@@ -221,11 +219,10 @@
                 add(chosen[:, :384], 0, 6, f)
 
         def add_diagonal(part):
-            came(part, "cd0", "cd1")
+            came(part, *(("cd0", "cd1") if part == late else ("cd",)))
             for f in range(*part):
                 add(chosen[:, 384:], 6, 2, f)
 
-        early, late = (0, FIELDS - 1), (FIELDS - 1, FIELDS)
         own(early)
         send_metas()
         average(FIELDS - 1)
@@ -334,7 +331,7 @@
     coarse = jnp.transpose(coarse_fields, (1, 0, 2))
     stay = pl.BlockSpec(memory_space=pl.ANY)
     vmem = pl.BlockSpec(memory_space=pltpu.VMEM)
-    copies = 22
+    copies = 21
     f32 = jnp.float32
     synced, sums = pl.pallas_call(
         functools.partial(kernel, blocks, slabs),
@@ -357,7 +354,7 @@
             pltpu.VMEM((EDGE, EDGE, EDGE, tile_count), f32),
             pltpu.VMEM((EDGE, EDGE, tile_count), f32),
             pltpu.VMEM((slabs, 2, EDGE, tile_count), f32),
-            pltpu.SemaphoreType.DMA((FIELDS * PIECES + 3 + FIELDS,)),
+            pltpu.SemaphoreType.DMA((FIELDS + 4,)),
             pltpu.SemaphoreType.DMA((blocks,)),
             pltpu.SemaphoreType.DMA((blocks,)),
             pltpu.SemaphoreType.DMA((copies,)),

time: 22.3 us -> 22.2 us (level)
  no operation moved by 1% of the time
where the time goes in v8:
time: 22.2 us; the launch traced here: 22 us
  Pallas kernels  21.4 us (96%)
  between operations  0.64 us (3%)
    pallas_call x1, Pallas kernels, shards(): pl.pallas_call(functools.partial(kernel, blocks, slabs), out_shape=(jax.S...  20.4 us
    pallas_call x1, Pallas kernels, shards(): pl.pallas_call(functools.partial(finish, slabs), out_shape=(jax.ShapeDtyp...  0.98 us

profile of v8, /device:TPU:0, one launch (start us, length us, event | category | flops | bytes accessed | tf_op | source)
XLA Modules:
  0.0 22.0 jit_solution(13763773476621682972)
XLA Ops:
  0.6 20.4 %average_down.1 = (f32[3,128,512]{2,1,0:T(8,128)S(1)}, f32[2,8,128]{2,1,0:T(8,128)S(1)}) custom-call(f32[3,128,512]{2,1,0:T(8,128)} %bitcast.4, f32[32,3,8,512]{3,2,1,0:T(8,128)} %fine_hbm.1, s32[1,32]{1,0:T(1,128)} %bitcast.5, s32[1,32]{1,0:T(1,128)} %bitcast.6, s32[128,512]{1,0:T(8,128)} %tags_hbm.1), custom_call_target="tpu_custom_call" | custom-call | tf_op jit(solution)/shard_map/average_down/pallas_call | solution.py:336
  21.1 1.0 %write_outputs.1 = (f32[3,128,512]{2,1,0:T(8,128)}, f32[1,1032]{1,0:T(1,128)}) custom-call(f32[3,128,512]{2,1,0:T(8,128)S(1)} %get-tuple-element.6.synced_in, f32[2,8,128]{2,1,0:T(8,128)S(1)} %get-tuple-element.7.sums), custom_call_target="tpu_custom_call" | custom-call | tf_op jit(solution)/shard_map/write_outputs/pallas_call | solution.py:374

commit v9 on v8

--- a/solution.py
+++ b/solution.py
@@ -206,8 +206,7 @@
             else:
                 go("cd", 6, 0, 2, 1, 7, part)
 
-        def drain(part, *later):
-            kept = [copies[name, part] for name in later if (name, part) in copies]
+        def drain(*kept):
             for copy in started:
                 if not any(copy is other for other in kept):
                     copy.wait_send()
@@ -236,9 +235,9 @@
         add_near(early)
         share_diagonal(early)
         add_near(late)
+        drain(copies["cd", early], copies["d0", late], copies["d1", late])
+        share_diagonal(late)
         add_diagonal(early)
-        drain(late, "d0", "d1")
-        share_diagonal(late)
         for f in range(*early):
             weigh(f)
         add_diagonal(late)

time: 22.2 us -> 21.7 us (0.977)
  Pallas kernels: 21.4 us -> 20.9 us
    pallas_call x1, Pallas kernels: 20.4 us -> 20 us  [shards(): pl.pallas_call(functools.partial(kernel, blocks, slabs), out_shape=(jax.S...]
where the time goes in v9:
time: 21.7 us; the launch traced here: 21.6 us
  Pallas kernels  20.9 us (96%)
  between operations  0.64 us (3%)
    pallas_call x1, Pallas kernels, shards(): pl.pallas_call(functools.partial(kernel, blocks, slabs), out_shape=(jax.S...  20 us
    pallas_call x1, Pallas kernels, shards(): pl.pallas_call(functools.partial(finish, slabs), out_shape=(jax.ShapeDtyp...  0.98 us

profile of v9, /device:TPU:0, one launch (start us, length us, event | category | flops | bytes accessed | tf_op | source)
XLA Modules:
  0.0 21.6 jit_solution(6595363459141715282)
XLA Ops:
  0.6 20.0 %average_down.1 = (f32[3,128,512]{2,1,0:T(8,128)S(1)}, f32[2,8,128]{2,1,0:T(8,128)S(1)}) custom-call(f32[3,128,512]{2,1,0:T(8,128)} %bitcast.4, f32[32,3,8,512]{3,2,1,0:T(8,128)} %fine_hbm.1, s32[1,32]{1,0:T(1,128)} %bitcast.5, s32[1,32]{1,0:T(1,128)} %bitcast.6, s32[128,512]{1,0:T(8,128)} %tags_hbm.1), custom_call_target="tpu_custom_call" | custom-call | tf_op jit(solution)/shard_map/average_down/pallas_call | solution.py:335
  20.6 1.0 %write_outputs.1 = (f32[3,128,512]{2,1,0:T(8,128)}, f32[1,1032]{1,0:T(1,128)}) custom-call(f32[3,128,512]{2,1,0:T(8,128)S(1)} %get-tuple-element.6.synced_in, f32[2,8,128]{2,1,0:T(8,128)S(1)} %get-tuple-element.7.sums), custom_call_target="tpu_custom_call" | custom-call | tf_op jit(solution)/shard_map/write_outputs/pallas_call | solution.py:373
